TPU v7x, 32 devices: a whole 2x2x4 slice. The times are simulated.
32 devices in a mesh: sh: 4 (over z), sw: 4 (over y, core), tp: 2 (over x).
Axes of the slice: x: 2, y: 2, z: 4, core: 2. Of those that a mesh axis runs over, the one named last changes fastest.
Arguments:
- queries: bfloat16 [2, 32, 32, 1536], P('tp', 'sh', 'sw'), may hold values from -6 to 6
- keys: bfloat16 [2, 32, 32, 1536], P('tp', 'sh', 'sw'), may hold values from -6 to 6
- values: bfloat16 [2, 32, 32, 1536], P('tp', 'sh', 'sw'), may hold values from -6 to 6
- attn_out: bfloat16 [2, 32, 32, 1536], P('tp', 'sh', 'sw'), may hold values from -6 to 6
- attn_grad: bfloat16 [2, 32, 32, 1536], P('tp', 'sh', 'sw'), may hold values from -192 to 192
- log_sum: float32 [2, 32, 32, 12], P('tp', 'sh', 'sw'), may hold values from 6.1 to 6.9
- window_dirs: int32 [12, 4], replicated, may hold values from 0 to 7, as said below
Outputs:
- q_grad: bfloat16 [2, 32, 32, 1536], P('tp', 'sh', 'sw')
- k_grad: bfloat16 [2, 32, 32, 1536], P('tp', 'sh', 'sw')
- v_grad: bfloat16 [2, 32, 32, 1536], P('tp', 'sh', 'sw')
Inputs may be any that keep to these rules, and one draw needn't show every extreme that they name: `window_dirs`: each row names 4 different directions. Within each run of 6 consecutive heads (those of one index of tp) every direction is named by exactly half of the rows.
All inputs are finite; a program needn't handle non-finite values.
Results may differ from a plain program's by a relative error of at most 0.0056.
Values may be sent and summed in bfloat16 or wider, within the bound.
A program may use at most 64 MiB of HBM per device.

v0:
```python
import functools

import jax
import jax.numpy as jnp
from jax import lax
from jax.experimental import pallas as pl
from jax.experimental.pallas import tpu as pltpu
from jax.sharding import PartitionSpec as P

E_OF = (1, 7, 4, 0, 3, 2, 8, 5)
BF = jnp.bfloat16
F32 = jnp.float32
NT = (((1,), (1,)), ((), ()))
TN = (((0,), (0,)), ((), ()))


def kernel(
    n_sh, n_sw, half, hd,
    q_in, k_in, v_in, g_in, o_in, lse_in, wd_in,
    dq_out, dk_out, dv_out,
    zb00, zb01, zb10, zb11, kv0, kv1, qg, pieces, packed, stats,
    q_ref, k_ref, v_ref, g_ref, o_ref, lse_ref, wd_ref, in_sem,
    rs00, rs01, rs02, rs10, rs11, rs12, dqs, dkp, own_kv, own_q,
    zsend, zback, xsend, xback, head_of, rank_of, member_of, flat_of,
    zs, zr, zts, ztr, xs, xr, ws, wr, wts, wtr, rs, rr, rzs, rzr, rxs, rxr,
):
    row = lax.axis_index("sh")
    col = lax.axis_index("sw")
    part = lax.axis_index("tp")
    zb = ((zb00, zb01), (zb10, zb11))
    kv = (kv0, kv1)
    rsw = ((rs00, rs01, rs02), (rs10, rs11, rs12))
    third = half // 2
    tok = q_ref.shape[0]
    arguments = (
        (q_in, q_ref), (g_in, g_ref), (k_in, k_ref), (v_in, v_ref), (wd_in, wd_ref), (o_in, o_ref), (lse_in, lse_ref),
    )
    loads = [pltpu.make_async_copy(src, dst, in_sem.at[i]) for i, (src, dst) in enumerate(arguments)]
    for load in loads:
        load.start()
    scale = hd ** -0.5
    row_ok = lambda step: (row + step >= 0) & (row + step < n_sh)
    col_ok = lambda step: (col + step >= 0) & (col + step < n_sw)
    row_step = (0, -1, 1)
    col_step = (-1, 1)

    def remote(src, dst, ssem, rsem, device):
        return pltpu.make_async_remote_copy(
            src_ref=src, dst_ref=dst, send_sem=ssem, recv_sem=rsem,
            device_id=device, device_id_type=pl.DeviceIdType.MESH,
        )

    def copy_z(run, i):
        return remote(qg.at[run], zb[run][i], zs.at[run, i], zr.at[run, i], {"sh": row + 2 * i - 1})

    def copy_zstat(i):
        return remote(stats.at[6], stats.at[7 + i], zts.at[i], ztr.at[i], {"sh": row + 2 * i - 1})

    def copy_x(run):
        src = kv[run].at[:, :, pl.ds(0, tok)]
        dst = kv[run].at[:, :, pl.ds(tok, tok)]
        return remote(src, dst, xs.at[run], xr.at[run], {"tp": 1 - part})

    def copy_w(run, c, i):
        e = c * 3 + i
        return remote(packed.at[run, e], pieces.at[run, e], ws.at[run, e], wr.at[run, e], {"sw": col + col_step[c]})

    def copy_wstat(c, i):
        e = c * 3 + i
        return remote(stats.at[6 + i], stats.at[e], wts.at[e], wtr.at[e], {"sw": col + col_step[c]})

    def copy_back(run, c, i):
        e = c * 3 + i
        return remote(dqs.at[run * 9 + e], rsw[run][i].at[c], rs.at[run, e], rr.at[run, e], {"sw": col - col_step[c]})

    def copy_zback(run, i):
        return remote(zsend.at[run, i], zback.at[run, i], rzs.at[run, i], rzr.at[run, i], {"sh": row - (2 * i - 1)})

    def copy_xback(run):
        return remote(xsend.at[run], xback.at[run], rxs.at[run], rxr.at[run], {"tp": 1 - part})

    barrier = pltpu.get_barrier_semaphore()
    pl.semaphore_signal(barrier, inc=1, device_id={"tp": 1 - part}, device_id_type=pl.DeviceIdType.MESH)
    for step in (-1, 1):
        @pl.when(row_ok(step))
        def _():
            pl.semaphore_signal(barrier, inc=1, device_id={"sh": row + step}, device_id_type=pl.DeviceIdType.MESH)

        @pl.when(col_ok(step))
        def _():
            pl.semaphore_signal(barrier, inc=1, device_id={"sw": col + step}, device_id_type=pl.DeviceIdType.MESH)
    count = 1
    for step in (-1, 1):
        count = count + row_ok(step).astype(jnp.int32) + col_ok(step).astype(jnp.int32)
    pl.semaphore_wait(barrier, count)

    loads[0].wait()
    loads[1].wait()
    for run in (0, 1):
        for h in range(half):
            cols = slice((run * half + h) * hd, (run * half + h + 1) * hd)
            qg[run, 0, h] = q_ref[:, cols]
            qg[run, 1, h] = g_ref[:, cols]
        for i in (0, 1):
            @pl.when(row_ok(2 * i - 1))
            def _():
                copy_z(run, i).start()
    loads[2].wait()
    loads[3].wait()
    for run in (0, 1):
        for h in range(half):
            cols = slice((run * half + h) * hd, (run * half + h + 1) * hd)
            kv[run][0, h, :tok] = k_ref[:, cols]
            kv[run][1, h, :tok] = v_ref[:, cols]
        copy_x(run).start()

    loads[4].wait()
    for run in (0, 1):
        dirs = [[wd_ref[j, run * half + h] for j in range(4)] for h in range(half)]
        flat = [[jnp.int32(0) for j in range(4)] for h in range(half)]
        for d in range(8):
            e = E_OF[d]
            seen = jnp.int32(0)
            heads = [jnp.int32(0) for _ in range(third)]
            for h in range(half):
                named = [(dirs[h][j] == d).astype(jnp.int32) for j in range(4)]
                member = named[0] + named[1] + named[2] + named[3]
                rank = jnp.minimum(seen, third - 1)
                rank_of[(run * 9 + e) * half + h] = rank
                member_of[(run * 9 + e) * half + h] = member
                at = (run * 9 + e) * third + rank
                for j in range(4):
                    flat[h][j] = flat[h][j] + named[j] * at
                for s in range(third):
                    heads[s] = heads[s] + member * (seen == s).astype(jnp.int32) * h
                seen = seen + member
            for s in range(third):
                head_of[(run * 9 + e) * third + s] = heads[s]
        for h in range(half):
            for j in range(4):
                flat_of[(run * half + h) * 4 + j] = flat[h][j]

    def pack(run, c, i):
        e = c * 3 + i
        for s in range(third):
            h = head_of[(run * 9 + e) * third + s]
            for a in (0, 1):
                block = qg[run, a, h] if i == 0 else zb[run][i - 1][a, h]
                if c == 2:
                    pieces[run, e, s, a] = block
                else:
                    packed[run, e, s, a] = block

    for run in (0, 1):
        for c in (0, 1):
            @pl.when(col_ok(col_step[c]))
            def _():
                pack(run, c, 0)
                copy_w(run, c, 0).start()

    loads[5].wait()
    loads[6].wait()
    lane = lax.broadcasted_iota(jnp.int32, (tok, hd), 1)
    table = jnp.zeros((tok, hd), F32)
    for run in (0, 1):
        for h in range(half):
            at = run * half + h
            cols = slice(at * hd, (at + 1) * hd)
            delta = jnp.sum(g_ref[:, cols].astype(F32) * o_ref[:, cols].astype(F32), axis=1, keepdims=True)
            table = jnp.where(lane == run * 16 + h, lse_ref[:, at:at + 1], table)
            table = jnp.where(lane == run * 16 + 8 + h, delta, table)
    square = jnp.concatenate([table, jnp.zeros((hd - tok, hd), F32)], axis=0) if tok < hd else table
    stats[6] = square.T[:32, :]
    for i in (0, 1):
        @pl.when(row_ok(2 * i - 1))
        def _():
            copy_zstat(i).start()
    for c in (0, 1):
        @pl.when(col_ok(col_step[c]))
        def _():
            copy_wstat(c, 0).start()

    def clear(e, carry):
        i = lax.rem(e, 3)
        c = lax.div(e, 3)
        r_step = jnp.where(i == 0, 0, 2 * i - 3)
        c_step = jnp.where(c == 2, 0, 2 * c - 1)
        live = row_ok(-r_step) & col_ok(-c_step)

        @pl.when(jnp.logical_not(live))
        def _():
            for run in (0, 1):
                for s in range(third):
                    dkp[(run * 9 + e) * third + s] = jnp.zeros(dkp.shape[1:], BF)
        return carry

    lax.fori_loop(0, 9, clear, 0)
    for c in (0, 1):
        @pl.when(jnp.logical_not(col_ok(col_step[c])))
        def _():
            for run in (0, 1):
                for i in range(3):
                    rsw[run][i][c] = jnp.zeros(rs00.shape[1:], BF)
    for i in (0, 1):
        @pl.when(jnp.logical_not(row_ok(2 * i - 1)))
        def _():
            for run in (0, 1):
                zback[run, i] = jnp.zeros(zback.shape[2:], BF)

    sub = lax.broadcasted_iota(jnp.int32, (8, hd), 0)

    def one(run, h, q, g, stat):
        keys = kv[run][0, h]
        vals = kv[run][1, h]
        pick = sub == h
        lse = jnp.sum(jnp.where(pick, stat[run * 16:run * 16 + 8], 0.0), axis=0, keepdims=True)[:, :tok]
        delta = jnp.sum(jnp.where(pick, stat[run * 16 + 8:run * 16 + 16], 0.0), axis=0, keepdims=True)[:, :tok]
        scores = lax.dot_general(keys, q, NT, preferred_element_type=F32)
        prob = jnp.exp(scores * scale - lse)
        grad_prob = lax.dot_general(vals, g, NT, preferred_element_type=F32)
        score_bf = (prob * (grad_prob - delta)).astype(BF)
        prob_bf = prob.astype(BF)
        dv = jnp.dot(prob_bf, g, preferred_element_type=F32)
        dk = jnp.dot(score_bf, q, preferred_element_type=F32) * scale
        dq = lax.dot_general(score_bf, keys, TN, preferred_element_type=F32) * scale
        return dq, dk, dv

    def own(run):
        def body(t, carry):
            stat = stats[6]
            for u in range(3):
                h = t * 3 + u
                dq, dk, dv = one(run, h, qg[run, 0, h], qg[run, 1, h], stat)
                own_q[run * half + h] = dq
                own_kv[run * half + h, 0] = dk
                own_kv[run * half + h, 1] = dv
            return carry

        lax.fori_loop(0, half // 3, body, 0)

    def group(run, e):
        stat = stats[e]
        for s in range(third):
            h = head_of[(run * 9 + e) * third + s]
            dq, dk, dv = one(run, h, pieces[run, e, s, 0], pieces[run, e, s, 1], stat)
            dqs[run * 9 + e, s] = dq.astype(BF)
            dkp[(run * 9 + e) * third + s, 0] = dk.astype(BF)
            dkp[(run * 9 + e) * third + s, 1] = dv.astype(BF)

    def from_side(run, c, i):
        @pl.when(row_ok(-row_step[i]) & col_ok(-col_step[c]))
        def _():
            copy_w(run, c, i).wait_recv()
            if run == 0:
                copy_wstat(c, i).wait_recv()
            group(run, c * 3 + i)
            copy_back(run, c, i).start()

    def relay(run):
        for i in (1, 2):
            @pl.when(row_ok(-row_step[i]))
            def _():
                copy_z(run, i - 1).wait_recv()
                if run == 0:
                    copy_zstat(i - 1).wait_recv()
                for c in (0, 1):
                    @pl.when(col_ok(col_step[c]))
                    def _():
                        pack(run, c, i)
                        copy_w(run, c, i).start()
                        if run == 0:
                            copy_wstat(c, i).start()
                pack(run, 2, i)

    def from_rows(run):
        for i in (1, 2):
            @pl.when(row_ok(-row_step[i]))
            def _():
                group(run, 6 + i)

    def wait_back(run, i):
        for c in (0, 1):
            @pl.when(row_ok(-row_step[i]) & col_ok(col_step[c]))
            def _():
                copy_back(run, c, i).wait_recv()

    def gathered(run, i, h, total):
        for c in (0, 1, 2):
            if c == 2 and i == 0:
                continue
            e = c * 3 + i
            rank = rank_of[(run * 9 + e) * half + h]
            held = dqs[run * 9 + e, rank] if c == 2 else rsw[run][i][c, rank]
            block = held.astype(F32) * member_of[(run * 9 + e) * half + h].astype(F32)
            total = block if total is None else total + block
        return total

    def turn(run):
        for i in (1, 2):
            @pl.when(row_ok(-row_step[i]))
            def _():
                wait_back(run, i)

                def body(h, carry):
                    zsend[run, i - 1, h] = gathered(run, i, h, None).astype(BF)
                    return carry

                lax.fori_loop(0, half, body, 0)
                copy_zback(run, i - 1).start()

    def total_kv(run, h, rows, a):
        total = own_kv[run * half + h, a, rows]
        for j in range(4):
            at = flat_of[(run * half + h) * 4 + j]
            total = total + dkp[at, a, rows].astype(F32)
        return total

    def to_partner(run):
        def body(h, carry):
            for a in (0, 1):
                xsend[run, a, h] = total_kv(run, h, slice(tok, 2 * tok), a).astype(BF)
            return carry

        lax.fori_loop(0, half, body, 0)
        copy_xback(run).start()

    def finish_kv(run):
        copy_xback(run).wait_recv()

        def body(h, carry):
            cols = pl.ds(pl.multiple_of((run * half + h) * hd, hd), hd)
            for a, out in ((0, dk_out), (1, dv_out)):
                total = total_kv(run, h, slice(0, tok), a) + xback[run, a, h].astype(F32)
                out[:, cols] = total.astype(BF)
            return carry

        lax.fori_loop(0, half, body, 0)

    def finish_q(run):
        wait_back(run, 0)
        for i in (0, 1):
            @pl.when(row_ok(2 * i - 1))
            def _():
                copy_zback(run, i).wait_recv()

        def body(h, carry):
            cols = pl.ds(pl.multiple_of((run * half + h) * hd, hd), hd)
            total = gathered(run, 0, h, own_q[run * half + h])
            total = total + zback[run, 0, h].astype(F32) + zback[run, 1, h].astype(F32)
            dq_out[:, cols] = total.astype(BF)
            return carry

        lax.fori_loop(0, half, body, 0)

    relay(0)
    copy_x(0).wait_recv()
    own(0)
    from_side(0, 0, 0)
    from_side(0, 1, 0)
    relay(1)
    from_rows(0)
    for i in (1, 2):
        for c in (0, 1):
            from_side(0, c, i)
    to_partner(0)
    copy_x(1).wait_recv()
    from_rows(1)
    turn(0)
    for i in (1, 2):
        for c in (0, 1):
            from_side(1, c, i)
    from_side(1, 0, 0)
    from_side(1, 1, 0)
    own(1)
    to_partner(1)
    turn(1)
    finish_kv(0)
    finish_q(0)
    finish_kv(1)
    finish_q(1)

    for run in (0, 1):
        copy_x(run).wait_send()
        copy_xback(run).wait_send()
        for i in (0, 1):
            @pl.when(row_ok(2 * i - 1))
            def _():
                copy_z(run, i).wait_send()
                if run == 0:
                    copy_zstat(i).wait_send()

            @pl.when(row_ok(1 - 2 * i))
            def _():
                copy_zback(run, i).wait_send()
        for c in (0, 1):
            for i in range(3):
                @pl.when(row_ok(-row_step[i]) & col_ok(col_step[c]))
                def _():
                    copy_w(run, c, i).wait_send()
                    if run == 0:
                        copy_wstat(c, i).wait_send()

                @pl.when(row_ok(-row_step[i]) & col_ok(-col_step[c]))
                def _():
                    copy_back(run, c, i).wait_send()


def hand_out(a_in, b_in, c_in, a_out, b_out, c_out, held, in_sem, out_sem):
    ins = [pltpu.make_async_copy(src, held.at[i], in_sem.at[i]) for i, src in enumerate((a_in, b_in, c_in))]
    outs = [pltpu.make_async_copy(held.at[i], dst, out_sem.at[i]) for i, dst in enumerate((a_out, b_out, c_out))]
    for copy in ins:
        copy.start()
    for first, second in zip(ins, outs):
        first.wait()
        second.start()
    for copy in outs:
        copy.wait()


def local(n_sh, n_sw, queries, keys, values, attn_out, attn_grad, log_sum, window_dirs):
    shape = queries.shape
    tok = shape[0] * shape[1] * shape[2]
    cols = shape[3]
    heads = log_sum.shape[3]
    half = heads // 2
    third = half // 2
    hd = cols // heads
    flat = lambda array: array.reshape(tok, array.shape[3])
    vmem = pl.BlockSpec(memory_space=pltpu.VMEM)
    hbm = pl.BlockSpec(memory_space=pltpu.HBM)
    dma = pltpu.SemaphoreType.DMA
    scratch = (
        [pltpu.VMEM((2, half, tok, hd), BF) for _ in range(4)]
        + [pltpu.VMEM((2, half, 2 * tok, hd), BF) for _ in range(2)]
        + [
            pltpu.VMEM((2, 2, half, tok, hd), BF),
            pltpu.VMEM((2, 9, third, 2, tok, hd), BF),
            pltpu.VMEM((2, 6, third, 2, tok, hd), BF),
            pltpu.VMEM((9, 32, hd), F32),
        ]
        + [pltpu.VMEM((tok, cols), BF) for _ in range(5)]
        + [pltpu.VMEM((tok, heads), F32), pltpu.SMEM((4, heads), jnp.int32), dma((7,))]
        + [pltpu.VMEM((2, third, tok, hd), BF) for _ in range(6)]
        + [
            pltpu.VMEM((18, third, tok, hd), BF),
            pltpu.VMEM((18 * third, 2, 2 * tok, hd), BF),
            pltpu.VMEM((heads, 2, 2 * tok, hd), F32),
            pltpu.VMEM((heads, tok, hd), F32),
            pltpu.VMEM((2, 2, half, tok, hd), BF),
            pltpu.VMEM((2, 2, half, tok, hd), BF),
            pltpu.VMEM((2, 2, half, tok, hd), BF),
            pltpu.VMEM((2, 2, half, tok, hd), BF),
            pltpu.SMEM((18 * third,), jnp.int32),
            pltpu.SMEM((18 * half,), jnp.int32),
            pltpu.SMEM((18 * half,), jnp.int32),
            pltpu.SMEM((heads * 4,), jnp.int32),
        ]
    )
    for sem in ((2, 2), (2,), (2,), (2, 6), (6,), (2, 6), (2, 2), (2,)):
        scratch += [dma(sem), dma(sem)]
    dq, dk, dv = pl.pallas_call(
        functools.partial(kernel, n_sh, n_sw, half, hd),
        out_shape=[jax.ShapeDtypeStruct((tok, cols), BF)] * 3,
        in_specs=[hbm] * 7,
        out_specs=[vmem] * 3,
        scratch_shapes=scratch,
        compiler_params=pltpu.CompilerParams(
            collective_id=0, has_side_effects=True, vmem_limit_bytes=64 * 2**20
        ),
    )(flat(queries), flat(keys), flat(values), flat(attn_grad), flat(attn_out), flat(log_sum), window_dirs.T)
    dq, dk, dv = pl.pallas_call(
        hand_out,
        out_shape=[jax.ShapeDtypeStruct((tok, cols), BF)] * 3,
        in_specs=[hbm] * 3,
        out_specs=[hbm] * 3,
        scratch_shapes=[pltpu.VMEM((3, tok, cols), BF), dma((3,)), dma((3,))],
        compiler_params=pltpu.CompilerParams(vmem_limit_bytes=64 * 2**20),
    )(dq, dk, dv)
    return tuple(array.reshape(shape) for array in (dq, dk, dv))


def solution(mesh):
    spec = P("tp", "sh", "sw", None)
    return jax.shard_map(
        functools.partial(local, mesh.shape["sh"], mesh.shape["sw"]),
        mesh=mesh,
        in_specs=(spec,) * 6 + (P(),),
        out_specs=(spec,) * 3,
        check_vma=False,
    )
```

profile of v0, /device:TPU:1, one launch (start us, length us, event | category | flops | bytes accessed | tf_op | source)
XLA Modules:
  0.0 38.6 jit_solution(10789330469647260417)
XLA Ops:
  0.6 36.1 %shard_map.94 = (bf16[64,1536]{1,0:T(8,128)(2,1)}, bf16[64,1536]{1,0:T(8,128)(2,1)}, bf16[64,1536]{1,0:T(8,128)(2,1)}) custom-call(bf16[64,1536]{1,0:T(8,128)(2,1)} %bitcast.10, bf16[64,1536]{1,0:T(8,128)(2,1)} %bitcast.11, bf16[64,1536]{1,0:T(8,128)(2,1)} %bitcast.12, bf16[64,1536]{1,0:T(8,128)(2,1)} %bitcast.13, bf16[64,1536]{1,0:T(8,128)(2,1)} %bitcast.14, ...), custom_call_target="tpu_custom_call" | custom-call | tf_op jit(solution)/shard_map/pallas_call | solution.py:461
  36.7 1.8 %shard_map.95 = (bf16[64,1536]{1,0:T(8,128)(2,1)}, bf16[64,1536]{1,0:T(8,128)(2,1)}, bf16[64,1536]{1,0:T(8,128)(2,1)}) custom-call(bf16[64,1536]{1,0:T(8,128)(2,1)} %get-tuple-element.9.a_in, bf16[64,1536]{1,0:T(8,128)(2,1)} %get-tuple-element.10.b_in, bf16[64,1536]{1,0:T(8,128)(2,1)} %get-tuple-element.11.c_in), custom_call_target="tpu_custom_call" | custom-call | tf_op jit(solution)/shard_map/pallas_call | solution.py:471
where the time goes:
time: 38.8 us; the launch traced here: 38.6 us
  Pallas kernels  37.9 us (98%)
  between operations  0.64 us (2%)
    pallas_call x1, Pallas kernels, local(): pl.pallas_call(functools.partial(kernel, n_sh, n_sw, half, hd), out_shape...  36.1 us
    pallas_call x1, Pallas kernels, local(): pl.pallas_call(hand_out, out_shape=[jax.ShapeDtypeStruct((tok, cols), BF)...  1.84 us

commit v1 on v0

v1 whole, which is shorter than its diff:
```python
import functools

import jax
import jax.numpy as jnp
from jax import lax
from jax.experimental import pallas as pl
from jax.experimental.pallas import tpu as pltpu
from jax.sharding import PartitionSpec as P

E_OF = (1, 7, 4, 0, 3, 2, 8, 5)
BF = jnp.bfloat16
F32 = jnp.float32
NT = (((1,), (1,)), ((), ()))
TN = (((0,), (0,)), ((), ()))


SIDES = (0, 1, 2, 3, 4, 5, 7, 8)
ROW_STEP = (0, -1, 1)
COL_STEP = (-1, 1, 0)


def kernel(
    n_sh, n_sw, half, hd,
    q_in, k_in, v_in, g_in, o_in, lse_in, wd_in,
    dq_out, dk_out, dv_out,
    kv0, kv1, qg, pieces0, pieces1, packed, stats,
    q_ref, k_ref, v_ref, g_ref, o_ref, lse_ref, wd_ref, in_sem,
    dqp, dqs, dqr0, dqr1, own_kv, own_q, xsend, xback,
    head_of, src_of, flat_of, e_of,
    zs, zr, zts, ztr, xs, xr, ws, wr, wts, wtr, bs, br, rxs, rxr, *zbs,
):
    row = lax.axis_index("sh")
    col = lax.axis_index("sw")
    part = lax.axis_index("tp")
    kv = (kv0, kv1)
    pieces = (pieces0, pieces1)
    dqr = (dqr0, dqr1)
    third = half // 2
    zb = [[zbs[(run * 2 + i) * third:(run * 2 + i + 1) * third] for i in (0, 1)] for run in (0, 1)]
    tok = q_ref.shape[0]
    arguments = (
        (q_in, q_ref), (g_in, g_ref), (k_in, k_ref), (v_in, v_ref), (wd_in, wd_ref), (o_in, o_ref), (lse_in, lse_ref),
    )
    loads = [pltpu.make_async_copy(src, dst, in_sem.at[i]) for i, (src, dst) in enumerate(arguments)]
    for load in loads:
        load.start()
    scale = hd ** -0.5
    row_ok = lambda step: (row + step >= 0) & (row + step < n_sh)
    col_ok = lambda step: (col + step >= 0) & (col + step < n_sw)
    spans = [(0, half - third + 1)] + [(half - third + k, half - third + k + 1) for k in range(1, third)]
    MESH = pl.DeviceIdType.MESH

    def sent_to(e):
        return row_ok(ROW_STEP[e % 3]) & col_ok(COL_STEP[e // 3])

    def came_from(e):
        return row_ok(-ROW_STEP[e % 3]) & col_ok(-COL_STEP[e // 3])

    def remote(src, dst, ssem, rsem, device):
        return pltpu.make_async_remote_copy(
            src_ref=src, dst_ref=dst, send_sem=ssem, recv_sem=rsem, device_id=device, device_id_type=MESH,
        )

    def copy_z(run, i, k):
        lo, hi = spans[k]
        return remote(
            qg.at[run, lo:hi], zb[run][i][k], zs.at[run, i, k], zr.at[run, i, k], {"sh": row + 2 * i - 1},
        )

    def copy_zstat(i):
        return remote(stats.at[6], stats.at[7 + i], zts.at[i], ztr.at[i], {"sh": row + 2 * i - 1})

    def copy_x(run):
        src = kv[run].at[:, :, pl.ds(0, tok)]
        dst = kv[run].at[:, :, pl.ds(tok, tok)]
        return remote(src, dst, xs.at[run], xr.at[run], {"tp": 1 - part})

    def copy_w(run, e, k):
        span = pl.ds(k, 1) if e % 3 else pl.ds(0, third)
        at = pl.ds(e * third + k, 1) if e % 3 else pl.ds(e * third, third)
        return remote(
            packed.at[run, e, span], pieces[run].at[at], ws.at[run, e, k], wr.at[run, e, k], {"sw": col + COL_STEP[e // 3]},
        )

    def copy_wstat(e):
        return remote(stats.at[6 + e % 3], stats.at[e], wts.at[e], wtr.at[e], {"sw": col + COL_STEP[e // 3]})

    def copy_back(run, e, k):
        at = run * 9 + e
        home = {"sh": row - ROW_STEP[e % 3], "sw": col - COL_STEP[e // 3]}
        return remote(dqs.at[at, k], dqr[run].at[e * third + k], bs.at[run, e, k], br.at[run, e, k], home)

    def copy_xback(run, k):
        lo, hi = spans[k]
        return remote(xsend.at[run, lo:hi], xback.at[run, lo:hi], rxs.at[run, k], rxr.at[run, k], {"tp": 1 - part})

    barrier = pltpu.get_barrier_semaphore()
    pl.semaphore_signal(barrier, inc=1, device_id={"tp": 1 - part}, device_id_type=MESH)
    count = 1
    for e in SIDES:
        @pl.when(sent_to(e))
        def _():
            near = {"sh": row + ROW_STEP[e % 3], "sw": col + COL_STEP[e // 3]}
            pl.semaphore_signal(barrier, inc=1, device_id=near, device_id_type=MESH)
        count = count + sent_to(e).astype(jnp.int32)

    loads[0].wait()
    loads[1].wait()
    for run in (0, 1):
        for h in range(half):
            cols = slice((run * half + h) * hd, (run * half + h + 1) * hd)
            qg[run, h, 0] = q_ref[:, cols]
            qg[run, h, 1] = g_ref[:, cols]
    pl.semaphore_wait(barrier, count)

    def send_z(run):
        for k in range(third):
            for i in (0, 1):
                @pl.when(row_ok(2 * i - 1))
                def _():
                    copy_z(run, i, k).start()

    send_z(0)
    loads[2].wait()
    loads[3].wait()
    for run in (0, 1):
        for h in range(half):
            cols = slice((run * half + h) * hd, (run * half + h + 1) * hd)
            kv[run][0, h, :tok] = k_ref[:, cols]
            kv[run][1, h, :tok] = v_ref[:, cols]
        copy_x(run).start()

    loads[4].wait()
    for run in (0, 1):
        dirs = [[wd_ref[j, run * half + h] for j in range(4)] for h in range(half)]
        flat = [[jnp.int32(0) for j in range(4)] for h in range(half)]
        tile = [[jnp.int32(0) for j in range(4)] for h in range(half)]
        for d in range(8):
            e = E_OF[d]
            seen = jnp.int32(0)
            heads = [jnp.int32(0) for _ in range(third)]
            srcs = [jnp.int32(0) for _ in range(third)]
            for h in range(half):
                named = [(dirs[h][j] == d).astype(jnp.int32) for j in range(4)]
                member = jnp.minimum(named[0] + named[1] + named[2] + named[3], 1)
                slot = jnp.minimum(named[1] + 2 * named[2] + 3 * named[3], 3) + (run * half + h) * 4
                at = e * third + jnp.minimum(seen, third - 1)
                for j in range(4):
                    flat[h][j] = flat[h][j] + named[j] * at
                    tile[h][j] = tile[h][j] + named[j] * e
                for s in range(third):
                    mine = member * (seen == s).astype(jnp.int32)
                    heads[s] = heads[s] + mine * h
                    srcs[s] = srcs[s] + mine * slot
                seen = seen + member
            for s in range(third):
                head_of[(run * 9 + e) * third + s] = heads[s]
                src_of[(run * 9 + e) * third + s] = srcs[s]
        for h in range(half):
            for j in range(4):
                flat_of[(run * half + h) * 4 + j] = flat[h][j]
                e_of[(run * half + h) * 4 + j] = tile[h][j]

    def pack(run, e, s):
        i = e % 3
        h = head_of[(run * 9 + e) * third + s]
        if i == 0:
            block = qg[run, h]
        else:
            held = zb[run][i - 1]
            block = held[0][jnp.minimum(h, spans[0][1] - 1)]
            for k in range(1, s + 1):
                block = jnp.where(h == spans[k][0], held[k][0], block)
        if e // 3 == 2:
            pieces[run][e * third + s] = block
        else:
            packed[run, e, s] = block

    for run in (0, 1):
        for e in (0, 3):
            @pl.when(sent_to(e))
            def _():
                for s in range(third):
                    pack(run, e, s)
                copy_w(run, e, 0).start()

    loads[5].wait()
    loads[6].wait()
    lane = lax.broadcasted_iota(jnp.int32, (tok, hd), 1)
    table = jnp.zeros((tok, hd), F32)
    for at in range(2 * half):
        cols = slice(at * hd, (at + 1) * hd)
        delta = jnp.sum(g_ref[:, cols].astype(F32) * o_ref[:, cols].astype(F32), axis=1, keepdims=True)
        table = jnp.where(lane == at, lse_ref[:, at:at + 1], table)
        table = jnp.where(lane == 16 + at, delta, table)
    turned = jnp.concatenate([table, jnp.zeros((hd - tok, hd), F32)], axis=0).T
    stats[6] = turned[:16] + pltpu.roll(turned[16:32], tok, 1)
    for i in (0, 1):
        @pl.when(row_ok(2 * i - 1))
        def _():
            copy_zstat(i).start()
    for e in (0, 3):
        @pl.when(sent_to(e))
        def _():
            copy_wstat(e).start()
    send_z(1)

    for e in SIDES:
        @pl.when(jnp.logical_not(came_from(e)))
        def _():
            stats[e] = jnp.zeros(stats.shape[1:], F32)
            for run in (0, 1):
                pieces[run][e * third:(e + 1) * third] = jnp.zeros((third,) + pieces0.shape[1:], BF)

        @pl.when(jnp.logical_not(sent_to(e)))
        def _():
            for run in (0, 1):
                dqr[run][e * third:(e + 1) * third] = jnp.zeros((third,) + dqr0.shape[1:], BF)

    def relay(run, k):
        for i in (1, 2):
            @pl.when(row_ok(-ROW_STEP[i]))
            def _():
                copy_z(run, i - 1, k).wait_recv()
                if run == 0 and k == third - 1:
                    copy_zstat(i - 1).wait_recv()
                for e in (i, 3 + i):
                    @pl.when(col_ok(COL_STEP[e // 3]))
                    def _():
                        pack(run, e, k)
                        copy_w(run, e, k).start()
                        if run == 0 and k == third - 1:
                            copy_wstat(e).start()
                pack(run, 6 + i, k)

    def products(keys, vals, q, g, lse, delta):
        scores = lax.dot_general(keys, q, NT, preferred_element_type=F32)
        prob = jnp.exp(scores * scale - lse)
        grad_prob = lax.dot_general(vals, g, NT, preferred_element_type=F32)
        score_bf = (prob * (grad_prob - delta)).astype(BF)
        dv = jnp.dot(prob.astype(BF), g, preferred_element_type=F32)
        dk = jnp.dot(score_bf, q, preferred_element_type=F32) * scale
        dq = lax.dot_general(score_bf, keys, TN, preferred_element_type=F32) * scale
        return dq, dk, dv

    def own(run):
        for h in range(half):
            at = run * half + h
            stat = stats[6, at:at + 1, :]
            dq, dk, dv = products(
                kv[run][0, h], kv[run][1, h], qg[run, h, 0], qg[run, h, 1], stat[:, :tok], pltpu.roll(stat, tok, 1)[:, :tok],
            )
            own_q[at] = dq
            own_kv[at, 0] = dk
            own_kv[at, 1] = dv

    first = lax.broadcasted_iota(jnp.int32, (1, hd), 1) < tok

    def near(run, h):
        at = run * half + h
        where = [flat_of[at * 4 + j] for j in range(4)]
        q = jnp.concatenate([pieces[run][w, 0] for w in where], axis=0)
        g = jnp.concatenate([pieces[run][w, 1] for w in where], axis=0)
        stat = [stats[e_of[at * 4 + j], at:at + 1, :] for j in range(4)]
        turn = [pltpu.roll(s, tok, 1) for s in stat]
        lse = jnp.concatenate([jnp.where(first, stat[j], turn[j + 1]) for j in (0, 2)], axis=1)
        delta = jnp.concatenate([jnp.where(first, turn[j], stat[j + 1]) for j in (0, 2)], axis=1)
        dq, dk, dv = products(kv[run][0, h], kv[run][1, h], q, g, lse, delta)
        for j in range(4):
            dqp[at * 4 + j] = dq[j * tok:(j + 1) * tok].astype(BF)
        for a, grad in ((0, dk), (1, dv)):
            total = own_kv[at, a] + grad
            own_kv[at, a, :tok] = total[:tok]
            xsend[run, h, a] = total[tok:].astype(BF)

    def arrived(run):
        for e in range(6):
            @pl.when(came_from(e))
            def _():
                for k in range(third if e % 3 else 1):
                    copy_w(run, e, k).wait_recv()
                if run == 0:
                    copy_wstat(e).wait_recv()

    def batch(run, k):
        for h in range(*spans[k]):
            near(run, h)
        copy_xback(run, k).start()
        for e in SIDES:
            dqs[run * 9 + e, k] = dqp[src_of[(run * 9 + e) * third + k]]

            @pl.when(came_from(e))
            def _():
                copy_back(run, e, k).start()

    def finish_kv(run, k):
        copy_xback(run, k).wait_recv()
        for h in range(*spans[k]):
            cols = slice((run * half + h) * hd, (run * half + h + 1) * hd)
            for a, out in ((0, dk_out), (1, dv_out)):
                out[:, cols] = (own_kv[run * half + h, a, :tok] + xback[run, h, a].astype(F32)).astype(BF)

    def finish_q(run):
        for e in SIDES:
            @pl.when(sent_to(e))
            def _():
                for k in range(third):
                    copy_back(run, e, k).wait_recv()
        for h in range(half):
            at = run * half + h
            total = own_q[at]
            for j in range(4):
                total = total + dqr[run][flat_of[at * 4 + j]].astype(F32)
            dq_out[:, at * hd:(at + 1) * hd] = total.astype(BF)

    for k in range(third):
        relay(0, k)
    copy_x(0).wait_recv()
    own(0)
    relay(1, 0)
    arrived(0)
    for k in range(third):
        batch(0, k)
    for k in range(1, third):
        relay(1, k)
    copy_x(1).wait_recv()
    own(1)
    arrived(1)
    for k in range(third):
        batch(1, k)
    for k in range(third):
        finish_kv(0, k)
    finish_q(0)
    for k in range(third):
        finish_kv(1, k)
    finish_q(1)
    for run in (0, 1):
        copy_x(run).wait_send()
        for k in range(third):
            copy_xback(run, k).wait_send()
            for i in (0, 1):
                @pl.when(row_ok(2 * i - 1))
                def _():
                    copy_z(run, i, k).wait_send()
                    if run == 0 and k == 0:
                        copy_zstat(i).wait_send()
            for e in range(6):
                @pl.when(row_ok(-ROW_STEP[e % 3]) & col_ok(COL_STEP[e // 3]))
                def _():
                    if e % 3 or k == 0:
                        copy_w(run, e, k).wait_send()
                    if run == 0 and k == 0:
                        copy_wstat(e).wait_send()
            for e in SIDES:
                @pl.when(came_from(e))
                def _():
                    copy_back(run, e, k).wait_send()


def hand_out(a_in, b_in, c_in, a_out, b_out, c_out, held, in_sem, out_sem):
    ins = [pltpu.make_async_copy(src, held.at[i], in_sem.at[i]) for i, src in enumerate((a_in, b_in, c_in))]
    outs = [pltpu.make_async_copy(held.at[i], dst, out_sem.at[i]) for i, dst in enumerate((a_out, b_out, c_out))]
    for copy in ins:
        copy.start()
    for first, second in zip(ins, outs):
        first.wait()
        second.start()
    for copy in outs:
        copy.wait()


def local(n_sh, n_sw, queries, keys, values, attn_out, attn_grad, log_sum, window_dirs):
    shape = queries.shape
    tok = shape[0] * shape[1] * shape[2]
    cols = shape[3]
    heads = log_sum.shape[3]
    half = heads // 2
    third = half // 2
    hd = cols // heads
    flat = lambda array: array.reshape(tok, array.shape[3])
    vmem = pl.BlockSpec(memory_space=pltpu.VMEM)
    hbm = pl.BlockSpec(memory_space=pltpu.HBM)
    dma = pltpu.SemaphoreType.DMA
    scratch = (
        [pltpu.VMEM((2, half, 2 * tok, hd), BF) for _ in range(2)]
        + [
            pltpu.VMEM((2, half, 2, tok, hd), BF),
            pltpu.VMEM((9 * third, 2, tok, hd), BF),
            pltpu.VMEM((9 * third, 2, tok, hd), BF),
            pltpu.VMEM((2, 6, third, 2, tok, hd), BF),
            pltpu.VMEM((9, 16, hd), F32),
        ]
        + [pltpu.VMEM((tok, cols), BF) for _ in range(5)]
        + [pltpu.VMEM((tok, heads), F32), pltpu.SMEM((4, heads), jnp.int32), dma((7,))]
        + [
            pltpu.VMEM((heads * 4, tok, hd), BF),
            pltpu.VMEM((18, third, tok, hd), BF),
            pltpu.VMEM((9 * third, tok, hd), BF),
            pltpu.VMEM((9 * third, tok, hd), BF),
            pltpu.VMEM((heads, 2, 2 * tok, hd), F32),
            pltpu.VMEM((heads, tok, hd), F32),
            pltpu.VMEM((2, half, 2, tok, hd), BF),
            pltpu.VMEM((2, half, 2, tok, hd), BF),
            pltpu.SMEM((18 * third,), jnp.int32),
            pltpu.SMEM((18 * third,), jnp.int32),
            pltpu.SMEM((heads * 4,), jnp.int32),
            pltpu.SMEM((heads * 4,), jnp.int32),
        ]
    )
    for sem in ((2, 2, third), (2,), (2,), (2, 6, third), (6,), (2, 9, third), (2, third)):
        scratch += [dma(sem), dma(sem)]
    for _ in range(4):
        scratch += [pltpu.VMEM((half - third + 1 if k == 0 else 1, 2, tok, hd), BF) for k in range(third)]
    dq, dk, dv = pl.pallas_call(
        functools.partial(kernel, n_sh, n_sw, half, hd),
        out_shape=[jax.ShapeDtypeStruct((tok, cols), BF)] * 3,
        in_specs=[hbm] * 7,
        out_specs=[vmem] * 3,
        scratch_shapes=scratch,
        compiler_params=pltpu.CompilerParams(
            collective_id=0, has_side_effects=True, vmem_limit_bytes=64 * 2**20
        ),
    )(flat(queries), flat(keys), flat(values), flat(attn_grad), flat(attn_out), flat(log_sum), window_dirs.T)
    dq, dk, dv = pl.pallas_call(
        hand_out,
        out_shape=[jax.ShapeDtypeStruct((tok, cols), BF)] * 3,
        in_specs=[hbm] * 3,
        out_specs=[hbm] * 3,
        scratch_shapes=[pltpu.VMEM((3, tok, cols), BF), dma((3,)), dma((3,))],
        compiler_params=pltpu.CompilerParams(vmem_limit_bytes=64 * 2**20),
    )(dq, dk, dv)
    return tuple(array.reshape(shape) for array in (dq, dk, dv))


def solution(mesh):
    spec = P("tp", "sh", "sw", None)
    return jax.shard_map(
        functools.partial(local, mesh.shape["sh"], mesh.shape["sw"]),
        mesh=mesh,
        in_specs=(spec,) * 6 + (P(),),
        out_specs=(spec,) * 3,
        check_vma=False,
    )
```

time: 38.8 us -> 32.1 us (0.83)
  Pallas kernels: 37.9 us -> 31.3 us
    pallas_call x1, Pallas kernels: 36.1 us -> 29.4 us  [local(): pl.pallas_call(functools.partial(kernel, n_sh, n_sw, half, hd), out_shape...]
where the time goes in v1:
time: 32.1 us; the launch traced here: 31.9 us
  Pallas kernels  31.3 us (98%)
  between operations  0.64 us (2%)
    pallas_call x1, Pallas kernels, local(): pl.pallas_call(functools.partial(kernel, n_sh, n_sw, half, hd), out_shape...  29.4 us
    pallas_call x1, Pallas kernels, local(): pl.pallas_call(hand_out, out_shape=[jax.ShapeDtypeStruct((tok, cols), BF)...  1.84 us

profile of v1, /device:TPU:1, one launch (start us, length us, event | category | flops | bytes accessed | tf_op | source)
XLA Modules:
  0.0 31.9 jit_solution(7093262702683550220)
XLA Ops:
  0.6 29.4 %shard_map.94 = (bf16[64,1536]{1,0:T(8,128)(2,1)}, bf16[64,1536]{1,0:T(8,128)(2,1)}, bf16[64,1536]{1,0:T(8,128)(2,1)}) custom-call(bf16[64,1536]{1,0:T(8,128)(2,1)} %bitcast.10, bf16[64,1536]{1,0:T(8,128)(2,1)} %bitcast.11, bf16[64,1536]{1,0:T(8,128)(2,1)} %bitcast.12, bf16[64,1536]{1,0:T(8,128)(2,1)} %bitcast.13, bf16[64,1536]{1,0:T(8,128)(2,1)} %bitcast.14, ...), custom_call_target="tpu_custom_call" | custom-call | tf_op jit(solution)/shard_map/pallas_call | solution.py:414
  30.1 1.8 %shard_map.95 = (bf16[64,1536]{1,0:T(8,128)(2,1)}, bf16[64,1536]{1,0:T(8,128)(2,1)}, bf16[64,1536]{1,0:T(8,128)(2,1)}) custom-call(bf16[64,1536]{1,0:T(8,128)(2,1)} %get-tuple-element.9.a_in, bf16[64,1536]{1,0:T(8,128)(2,1)} %get-tuple-element.10.b_in, bf16[64,1536]{1,0:T(8,128)(2,1)} %get-tuple-element.11.c_in), custom_call_target="tpu_custom_call" | custom-call | tf_op jit(solution)/shard_map/pallas_call | solution.py:424

commit v2 on v1

--- a/solution.py
+++ b/solution.py
@@ -357,14 +357,13 @@
                     copy_back(run, e, k).wait_send()
 
 
-def hand_out(a_in, b_in, c_in, a_out, b_out, c_out, held, in_sem, out_sem):
-    ins = [pltpu.make_async_copy(src, held.at[i], in_sem.at[i]) for i, src in enumerate((a_in, b_in, c_in))]
-    outs = [pltpu.make_async_copy(held.at[i], dst, out_sem.at[i]) for i, dst in enumerate((a_out, b_out, c_out))]
-    for copy in ins:
+def hand_out(a_in, b_in, c_in, a_out, b_out, c_out, out_sem):
+    outs = [
+        pltpu.make_async_copy(src, dst, out_sem.at[i])
+        for i, (src, dst) in enumerate(((a_in, a_out), (b_in, b_out), (c_in, c_out)))
+    ]
+    for copy in outs:
         copy.start()
-    for first, second in zip(ins, outs):
-        first.wait()
-        second.start()
     for copy in outs:
         copy.wait()
 
@@ -377,7 +376,8 @@
     half = heads // 2
     third = half // 2
     hd = cols // heads
-    flat = lambda array: array.reshape(tok, array.shape[3])
+    place = pltpu.with_memory_space_constraint
+    flat = lambda array: place(array.reshape(tok, array.shape[3]), pltpu.HBM)
     vmem = pl.BlockSpec(memory_space=pltpu.VMEM)
     hbm = pl.BlockSpec(memory_space=pltpu.HBM)
     dma = pltpu.SemaphoreType.DMA
@@ -413,22 +413,21 @@
         scratch += [pltpu.VMEM((half - third + 1 if k == 0 else 1, 2, tok, hd), BF) for k in range(third)]
     dq, dk, dv = pl.pallas_call(
         functools.partial(kernel, n_sh, n_sw, half, hd),
-        out_shape=[jax.ShapeDtypeStruct((tok, cols), BF)] * 3,
+        out_shape=[pltpu.VMEM((tok, cols), BF)] * 3,
         in_specs=[hbm] * 7,
         out_specs=[vmem] * 3,
         scratch_shapes=scratch,
         compiler_params=pltpu.CompilerParams(
-            collective_id=0, has_side_effects=True, vmem_limit_bytes=64 * 2**20
+            collective_id=0, has_side_effects=True, vmem_limit_bytes=32 * 2**20
         ),
-    )(flat(queries), flat(keys), flat(values), flat(attn_grad), flat(attn_out), flat(log_sum), window_dirs.T)
+    )(flat(queries), flat(keys), flat(values), flat(attn_grad), flat(attn_out), flat(log_sum), place(window_dirs.T, pltpu.HBM))
     dq, dk, dv = pl.pallas_call(
         hand_out,
         out_shape=[jax.ShapeDtypeStruct((tok, cols), BF)] * 3,
-        in_specs=[hbm] * 3,
+        in_specs=[vmem] * 3,
         out_specs=[hbm] * 3,
-        scratch_shapes=[pltpu.VMEM((3, tok, cols), BF), dma((3,)), dma((3,))],
-        compiler_params=pltpu.CompilerParams(vmem_limit_bytes=64 * 2**20),
-    )(dq, dk, dv)
+        scratch_shapes=[dma((3,))],
+    )(*(place(array, pltpu.VMEM) for array in (dq, dk, dv)))
     return tuple(array.reshape(shape) for array in (dq, dk, dv))
 
 

time: 32.1 us -> 30.3 us (0.944)
  Pallas kernels: 31.3 us -> 29.5 us
    pallas_call x1, Pallas kernels: 1.84 us -> 0.83 us  [local(): pl.pallas_call(hand_out, out_shape=[jax.ShapeDtypeStruct((tok, cols), BF)...]
    pallas_call x1, Pallas kernels: 29.4 us -> 28.6 us  [local(): pl.pallas_call(functools.partial(kernel, n_sh, n_sw, half, hd), out_shape...]
where the time goes in v2:
time: 30.3 us; the launch traced here: 30.1 us
  Pallas kernels  29.5 us (97%)
  between operations  0.64 us (2%)
    pallas_call x1, Pallas kernels, local(): pl.pallas_call(functools.partial(kernel, n_sh, n_sw, half, hd), out_shape...  28.6 us
    pallas_call x1, Pallas kernels, local(): pl.pallas_call(hand_out, out_shape=[jax.ShapeDtypeStruct((tok, cols), BF)...  0.83 us

profile of v2, /device:TPU:1, one launch (start us, length us, event | category | flops | bytes accessed | tf_op | source)
XLA Modules:
  0.0 30.1 jit_solution(7738547970239330062)
XLA Ops:
  0.6 28.6 %shard_map.94 = (bf16[64,1536]{1,0:T(8,128)(2,1)S(1)}, bf16[64,1536]{1,0:T(8,128)(2,1)S(1)}, bf16[64,1536]{1,0:T(8,128)(2,1)S(1)}) custom-call(bf16[64,1536]{1,0:T(8,128)(2,1)} %bitcast.10, bf16[64,1536]{1,0:T(8,128)(2,1)} %bitcast.11, bf16[64,1536]{1,0:T(8,128)(2,1)} %bitcast.12, bf16[64,1536]{1,0:T(8,128)(2,1)} %bitcast.13, bf16[64,1536]{1,0:T(8,128)(2,1)} %bitcast.14, ...), custom_call_target="tpu_custom_call" | custom-call | tf_op jit(solution)/shard_map/pallas_call | solution.py:414
  29.3 0.8 %shard_map.95 = (bf16[64,1536]{1,0:T(8,128)(2,1)}, bf16[64,1536]{1,0:T(8,128)(2,1)}, bf16[64,1536]{1,0:T(8,128)(2,1)}) custom-call(bf16[64,1536]{1,0:T(8,128)(2,1)S(1)} %get-tuple-element.9.a_in, bf16[64,1536]{1,0:T(8,128)(2,1)S(1)} %get-tuple-element.10.b_in, bf16[64,1536]{1,0:T(8,128)(2,1)S(1)} %get-tuple-element.11.c_in), custom_call_target="tpu_custom_call" | custom-call | tf_op jit(solution)/shard_map/pallas_call | solution.py:424

commit v3 on v2

v3 whole, which is shorter than its diff:
```python
import functools

import jax
import jax.numpy as jnp
from jax import lax
from jax.experimental import pallas as pl
from jax.experimental.pallas import tpu as pltpu
from jax.sharding import PartitionSpec as P

E_OF = (1, 7, 4, 0, 3, 2, 8, 5)
BF = jnp.bfloat16
F32 = jnp.float32
NT = (((1,), (1,)), ((), ()))
TN = (((0,), (0,)), ((), ()))


SIDES = (0, 1, 2, 3, 4, 5, 7, 8)
ROW_STEP = (0, -1, 1)
COL_STEP = (-1, 1, 0)


def kernel(
    n_sh, n_sw, half, hd,
    q_in, k_in, v_in, g_in, o_in, lse_in, wd_in,
    dq_out, dk_out, dv_out,
    kvx, qg, zq, pieces0, pieces1, packed, stats,
    q_ref, k_ref, v_ref, g_ref, o_ref, lse_ref, wd_ref, in_sem,
    dqp, dqs, dqr0, dqr1, own_kv, own_q, xsend, xback,
    head_of, src_of, flat_of, e_of,
    zs, zr, zts, ztr, xs, xr, ws, wr, wts, wtr, bs, br, rxr, *zbs,
):
    row = lax.axis_index("sh")
    col = lax.axis_index("sw")
    part = lax.axis_index("tp")
    pieces = (pieces0, pieces1)
    dqr = (dqr0, dqr1)
    third = half // 2
    zb = [[zbs[(run * 2 + i) * third:(run * 2 + i + 1) * third] for i in (0, 1)] for run in (0, 1)]
    tok = q_ref.shape[0]
    arguments = (
        (q_in, q_ref), (g_in, g_ref), (k_in, k_ref), (v_in, v_ref), (wd_in, wd_ref), (o_in, o_ref), (lse_in, lse_ref),
    )
    loads = [pltpu.make_async_copy(src, dst, in_sem.at[i]) for i, (src, dst) in enumerate(arguments)]
    for load in loads:
        load.start()
    scale = hd ** -0.5
    row_ok = lambda step: (row + step >= 0) & (row + step < n_sh)
    col_ok = lambda step: (col + step >= 0) & (col + step < n_sw)
    spans = [(0, half - third + 1)] + [(half - third + k, half - third + k + 1) for k in range(1, third)]
    MESH = pl.DeviceIdType.MESH

    def sent_to(e):
        return row_ok(ROW_STEP[e % 3]) & col_ok(COL_STEP[e // 3])

    def came_from(e):
        return row_ok(-ROW_STEP[e % 3]) & col_ok(-COL_STEP[e // 3])

    def remote(src, dst, ssem, rsem, device):
        return pltpu.make_async_remote_copy(
            src_ref=src, dst_ref=dst, send_sem=ssem, recv_sem=rsem, device_id=device, device_id_type=MESH,
        )

    def copy_z(run, i, k, a):
        lo, hi = ((run * half + h) * hd for h in spans[k])
        src = (q_in, g_in)[a].at[:, lo:hi]
        return remote(src, zb[run][i][k].at[a], zs.at[i], zr.at[run, i, k], {"sh": row + 2 * i - 1})

    def copy_zstat(i):
        return remote(stats.at[6], stats.at[7 + i], zts.at[i], ztr.at[i], {"sh": row + 2 * i - 1})

    def copy_x(run, a):
        cols = slice(run * half * hd, (run + 1) * half * hd)
        return remote((k_in, v_in)[a].at[:, cols], kvx.at[a, :, cols], xs.at[0], xr.at[run], {"tp": 1 - part})

    def copy_w(run, e, k):
        span = pl.ds(k, 1) if e % 3 else pl.ds(0, third)
        at = pl.ds(e * third + k, 1) if e % 3 else pl.ds(e * third, third)
        return remote(
            packed.at[run, e, span], pieces[run].at[at], ws.at[e // 3], wr.at[run, e // 3], {"sw": col + COL_STEP[e // 3]},
        )

    def copy_wstat(e):
        return remote(stats.at[6 + e % 3], stats.at[e], wts.at[e // 3], wtr.at[e // 3], {"sw": col + COL_STEP[e // 3]})

    def copy_back(run, e, k):
        at = run * 9 + e
        home = {"sh": row - ROW_STEP[e % 3], "sw": col - COL_STEP[e // 3]}
        return remote(dqs.at[at, k], dqr[run].at[e * third + k], bs.at[e % 3], br.at[run, e % 3], home)

    def copy_xback(run, h):
        return remote(xsend.at[run, h], xback.at[run, h], xs.at[0], rxr.at[run], {"tp": 1 - part})

    n_rows = row_ok(-1).astype(jnp.int32) + row_ok(1).astype(jnp.int32)
    n_cols = col_ok(-1).astype(jnp.int32) + col_ok(1).astype(jnp.int32)

    def drain(ref, sem):
        pltpu.make_async_copy(ref, ref, sem).wait()

    barrier = pltpu.get_barrier_semaphore()
    pl.semaphore_signal(barrier, inc=1, device_id={"tp": 1 - part}, device_id_type=MESH)
    count = 1
    for e in SIDES:
        @pl.when(sent_to(e))
        def _():
            near = {"sh": row + ROW_STEP[e % 3], "sw": col + COL_STEP[e // 3]}
            pl.semaphore_signal(barrier, inc=1, device_id=near, device_id_type=MESH)
        count = count + sent_to(e).astype(jnp.int32)

    pl.semaphore_wait(barrier, count)

    def send_z(run):
        for k in range(third):
            for i in (0, 1):
                @pl.when(row_ok(2 * i - 1))
                def _():
                    copy_z(run, i, k, 0).start()
                    copy_z(run, i, k, 1).start()

    send_z(0)
    for run in (0, 1):
        for a in (0, 1):
            copy_x(run, a).start()

    for i in (4, 0, 1, 5, 6):
        loads[i].wait()
    for run in (0, 1):
        seen = jnp.int32(0)
        heads = [jnp.int32(0) for _ in range(third)]
        slots = [jnp.int32(0) for _ in range(third)]
        for h in range(half):
            dirs = [wd_ref[j, run * half + h] for j in range(4)]
            bits = [(d & 1, (d >> 1) & 1, d >> 2) for d in dirs]
            one = [(1 + 15 * a) * (1 + 255 * b) * (1 + 65535 * c) for a, b, c in bits]
            for j in range(4):
                field = seen & (one[j] * 15)
                here = [field == one[j] * s for s in range(third)]
                rank = sum(here[s].astype(jnp.int32) * s for s in range(1, third))
                n = dirs[j] + bits[j][2]
                up = (n * 11) >> 5
                over = n - 3 * up
                e = jnp.where(over == 1, 6, jnp.where(over == 2, 3, 0)) + jnp.where(up == 1, 0, jnp.where(up == 2, 2, 1))
                flat_of[(run * half + h) * 4 + j] = e * third + rank
                e_of[(run * half + h) * 4 + j] = e
                for s in range(third):
                    mine = jnp.where(here[s], one[j], 0)
                    if h:
                        heads[s] = heads[s] + mine * h
                    if j:
                        slots[s] = slots[s] + mine * j
            seen = seen + (one[0] + one[1]) + (one[2] + one[3])
        for d in range(8):
            for s in range(third):
                h = jnp.minimum(lax.shift_right_logical(heads[s], 4 * d) & 15, half - 1)
                head_of[(run * 9 + E_OF[d]) * third + s] = h
                src_of[(run * 9 + E_OF[d]) * third + s] = (run * half + h) * 4 + jnp.minimum(lax.shift_right_logical(slots[s], 4 * d) & 15, 3)

    lane = lax.broadcasted_iota(jnp.int32, (tok, hd), 1)
    table = jnp.zeros((tok, hd), F32)
    for at in range(2 * half):
        cols = slice(at * hd, (at + 1) * hd)
        delta = jnp.sum(g_ref[:, cols].astype(F32) * o_ref[:, cols].astype(F32), axis=1, keepdims=True)
        table = jnp.where(lane == at, lse_ref[:, at:at + 1], table)
        table = jnp.where(lane == 16 + at, delta, table)
    turned = jnp.concatenate([table, jnp.zeros((hd - tok, hd), F32)], axis=0).T
    stats[6] = turned[:16] + pltpu.roll(turned[16:32], tok, 1)
    for i in (0, 1):
        @pl.when(row_ok(2 * i - 1))
        def _():
            copy_zstat(i).start()
    send_z(1)

    def pack(run, e, s):
        i = e % 3
        h = head_of[(run * 9 + e) * third + s]
        block = zq[run * 2 + i - 1, h] if i else qg[run, h]
        if e // 3 == 2:
            pieces[run][e * third + s] = block
        else:
            packed[run, e, s] = block

    for run in (0, 1):
        for h in range(half):
            cols = slice((run * half + h) * hd, (run * half + h + 1) * hd)
            qg[run, h, 0] = q_ref[:, cols]
            qg[run, h, 1] = g_ref[:, cols]
    for run in (0, 1):
        for e in (0, 3):
            @pl.when(sent_to(e))
            def _():
                for s in range(third):
                    pack(run, e, s)
                copy_w(run, e, 0).start()
    for e in (0, 3):
        @pl.when(sent_to(e))
        def _():
            copy_wstat(e).start()

    for e in SIDES:
        @pl.when(jnp.logical_not(came_from(e)))
        def _():
            stats[e] = jnp.zeros(stats.shape[1:], F32)
            for run in (0, 1):
                pieces[run][e * third:(e + 1) * third] = jnp.zeros((third,) + pieces0.shape[1:], BF)

        @pl.when(jnp.logical_not(sent_to(e)))
        def _():
            for run in (0, 1):
                dqr[run][e * third:(e + 1) * third] = jnp.zeros((third,) + dqr0.shape[1:], BF)

    def relay(run, k):
        for i in (1, 2):
            @pl.when(row_ok(-ROW_STEP[i]))
            def _():
                held = zb[run][i - 1][k]
                drain(held, zr.at[run, i - 1, k])
                for n, h in enumerate(range(*spans[k])):
                    for a in (0, 1):
                        zq[run * 2 + i - 1, h, a] = held[a, :, n * hd:(n + 1) * hd]
                if run == 0 and k == third - 1:
                    copy_zstat(i - 1).wait_recv()
                for e in (i, 3 + i):
                    @pl.when(col_ok(COL_STEP[e // 3]))
                    def _():
                        pack(run, e, k)
                        copy_w(run, e, k).start()
                        if run == 0 and k == third - 1:
                            copy_wstat(e).start()
                pack(run, 6 + i, k)

    def products(keys, vals, q, g, lse, delta):
        scores = lax.dot_general(keys, q, NT, preferred_element_type=F32)
        prob = jnp.exp(scores * scale - lse)
        grad_prob = lax.dot_general(vals, g, NT, preferred_element_type=F32)
        score_bf = (prob * (grad_prob - delta)).astype(BF)
        dv = jnp.dot(prob.astype(BF), g, preferred_element_type=F32)
        dk = jnp.dot(score_bf, q, preferred_element_type=F32) * scale
        dq = lax.dot_general(score_bf, keys, TN, preferred_element_type=F32) * scale
        return dq, dk, dv

    def keys_of(at):
        cols = slice(at * hd, (at + 1) * hd)
        return (jnp.concatenate([mine[:, cols], other[:, cols]], axis=0) for mine, other in ((k_ref, kvx.at[0]), (v_ref, kvx.at[1])))

    def own(run):
        for h in range(half):
            at = run * half + h
            cols = slice(at * hd, (at + 1) * hd)
            stat = stats[6, at:at + 1, :]
            dq, dk, dv = products(
                *keys_of(at), q_ref[:, cols], g_ref[:, cols], stat[:, :tok], pltpu.roll(stat, tok, 1)[:, :tok],
            )
            own_q[at] = dq
            own_kv[at, 0] = dk
            own_kv[at, 1] = dv

    first = lax.broadcasted_iota(jnp.int32, (1, hd), 1) < tok

    def near(run, h):
        at = run * half + h
        where = [flat_of[at * 4 + j] for j in range(4)]
        q = jnp.concatenate([pieces[run][w, 0] for w in where], axis=0)
        g = jnp.concatenate([pieces[run][w, 1] for w in where], axis=0)
        stat = [stats[e_of[at * 4 + j], at:at + 1, :] for j in range(4)]
        turn = [pltpu.roll(s, tok, 1) for s in stat]
        lse = jnp.concatenate([jnp.where(first, stat[j], turn[j + 1]) for j in (0, 2)], axis=1)
        delta = jnp.concatenate([jnp.where(first, turn[j], stat[j + 1]) for j in (0, 2)], axis=1)
        dq, dk, dv = products(*keys_of(at), q, g, lse, delta)
        for j in range(4):
            dqp[at * 4 + j] = dq[j * tok:(j + 1) * tok].astype(BF)
        for a, grad in ((0, dk), (1, dv)):
            total = own_kv[at, a] + grad
            own_kv[at, a, :tok] = total[:tok]
            xsend[run, h, a] = total[tok:].astype(BF)

    def arrived(run):
        for c in (0, 1):
            for v in (0, 1, 2):
                @pl.when(col_ok(-COL_STEP[c]) & (n_rows == v))
                def _():
                    drain(pieces[run].at[0:third * (1 + v)], wr.at[run, c])
                    if run == 0:
                        drain(stats.at[0:1 + v], wtr.at[c])

    def batch(run, k):
        for h in range(*spans[k]):
            near(run, h)
            copy_xback(run, h).start()
        for e in SIDES:
            dqs[run * 9 + e, k] = dqp[src_of[(run * 9 + e) * third + k]]

            @pl.when(came_from(e))
            def _():
                copy_back(run, e, k).start()

    def finish_kv(run):
        drain(xback.at[run], rxr.at[run])
        for h in range(half):
            cols = slice((run * half + h) * hd, (run * half + h + 1) * hd)
            for a, out in ((0, dk_out), (1, dv_out)):
                out[:, cols] = (own_kv[run * half + h, a, :tok] + xback[run, h, a].astype(F32)).astype(BF)

    def finish_q(run):
        for i in range(3):
            for v in (0, 1, 2):
                if v or i:
                    @pl.when(row_ok(ROW_STEP[i]) & (n_cols == v))
                    def _():
                        drain(dqr[run].at[0:third * (v + (i > 0))], br.at[run, i])
        for h in range(half):
            at = run * half + h
            total = own_q[at]
            for j in range(4):
                total = total + dqr[run][flat_of[at * 4 + j]].astype(F32)
            dq_out[:, at * hd:(at + 1) * hd] = total.astype(BF)

    def got_x(run):
        drain(kvx.at[:, :, run * half * hd:(run + 1) * half * hd], xr.at[run])

    loads[2].wait()
    loads[3].wait()
    for k in range(third):
        relay(0, k)
    got_x(0)
    own(0)
    relay(1, 0)
    arrived(0)
    for k in range(third):
        batch(0, k)
    for k in range(1, third):
        relay(1, k)
    got_x(1)
    own(1)
    arrived(1)
    for k in range(third):
        batch(1, k)
    finish_kv(0)
    finish_q(0)
    finish_kv(1)
    finish_q(1)

    drain(dqp, xs.at[0])
    for i in (0, 1):
        @pl.when(row_ok(2 * i - 1))
        def _():
            drain(dqp.at[0:4 * half], zs.at[i])
            copy_zstat(i).wait_send()
    for v in (0, 1, 2):
        for c in (0, 1):
            @pl.when(col_ok(COL_STEP[c]) & (n_rows == v))
            def _():
                drain(dqp.at[0:4 * third * (1 + v)], ws.at[c])
                drain(stats.at[0:1 + v], wts.at[c])
        for i in range(3):
            if v or i:
                @pl.when(row_ok(-ROW_STEP[i]) & (n_cols == v))
                def _():
                    drain(dqp.at[0:2 * third * (v + (i > 0))], bs.at[i])


def hand_out(a_in, b_in, c_in, a_out, b_out, c_out, out_sem):
    outs = [
        pltpu.make_async_copy(src, dst, out_sem.at[i])
        for i, (src, dst) in enumerate(((a_in, a_out), (b_in, b_out), (c_in, c_out)))
    ]
    for copy in outs:
        copy.start()
    for copy in outs:
        copy.wait()


def local(n_sh, n_sw, queries, keys, values, attn_out, attn_grad, log_sum, window_dirs):
    shape = queries.shape
    tok = shape[0] * shape[1] * shape[2]
    cols = shape[3]
    heads = log_sum.shape[3]
    half = heads // 2
    third = half // 2
    hd = cols // heads
    place = pltpu.with_memory_space_constraint
    flat = lambda array: place(array.reshape(tok, array.shape[3]), pltpu.HBM)
    vmem = pl.BlockSpec(memory_space=pltpu.VMEM)
    hbm = pl.BlockSpec(memory_space=pltpu.HBM)
    dma = pltpu.SemaphoreType.DMA
    scratch = (
        [
            pltpu.VMEM((2, tok, cols), BF),
            pltpu.VMEM((2, half, 2, tok, hd), BF),
            pltpu.VMEM((4, half, 2, tok, hd), BF),
        ]
        + [
            pltpu.VMEM((9 * third, 2, tok, hd), BF),
            pltpu.VMEM((9 * third, 2, tok, hd), BF),
            pltpu.VMEM((2, 6, third, 2, tok, hd), BF),
            pltpu.VMEM((9, 16, hd), F32),
        ]
        + [pltpu.VMEM((tok, cols), BF) for _ in range(5)]
        + [pltpu.VMEM((tok, heads), F32), pltpu.SMEM((4, heads), jnp.int32), dma((7,))]
        + [
            pltpu.VMEM((heads * 4, tok, hd), BF),
            pltpu.VMEM((18, third, tok, hd), BF),
            pltpu.VMEM((9 * third, tok, hd), BF),
            pltpu.VMEM((9 * third, tok, hd), BF),
            pltpu.VMEM((heads, 2, 2 * tok, hd), F32),
            pltpu.VMEM((heads, tok, hd), F32),
            pltpu.VMEM((2, half, 2, tok, hd), BF),
            pltpu.VMEM((2, half, 2, tok, hd), BF),
            pltpu.SMEM((18 * third,), jnp.int32),
            pltpu.SMEM((18 * third,), jnp.int32),
            pltpu.SMEM((heads * 4,), jnp.int32),
            pltpu.SMEM((heads * 4,), jnp.int32),
        ]
    )
    sems = ((2,), (2, 2, third), (2,), (2,), (1,), (2,), (2,), (2, 2), (2,), (2,), (3,), (2, 3), (2,))
    scratch += [dma(sem) for sem in sems]
    for _ in range(4):
        scratch += [pltpu.VMEM((2, tok, (half - third + 1 if k == 0 else 1) * hd), BF) for k in range(third)]
    dq, dk, dv = pl.pallas_call(
        functools.partial(kernel, n_sh, n_sw, half, hd),
        out_shape=[pltpu.VMEM((tok, cols), BF)] * 3,
        in_specs=[hbm] * 7,
        out_specs=[vmem] * 3,
        scratch_shapes=scratch,
        compiler_params=pltpu.CompilerParams(
            collective_id=0, has_side_effects=True, vmem_limit_bytes=32 * 2**20
        ),
    )(flat(queries), flat(keys), flat(values), flat(attn_grad), flat(attn_out), flat(log_sum), place(window_dirs.T, pltpu.HBM))
    dq, dk, dv = pl.pallas_call(
        hand_out,
        out_shape=[jax.ShapeDtypeStruct((tok, cols), BF)] * 3,
        in_specs=[vmem] * 3,
        out_specs=[hbm] * 3,
        scratch_shapes=[dma((3,))],
    )(*(place(array, pltpu.VMEM) for array in (dq, dk, dv)))
    return tuple(array.reshape(shape) for array in (dq, dk, dv))


def solution(mesh):
    spec = P("tp", "sh", "sw", None)
    return jax.shard_map(
        functools.partial(local, mesh.shape["sh"], mesh.shape["sw"]),
        mesh=mesh,
        in_specs=(spec,) * 6 + (P(),),
        out_specs=(spec,) * 3,
        check_vma=False,
    )
```

time: 30.3 us -> 29.6 us (0.977)
  Pallas kernels: 29.5 us -> 28.8 us
    pallas_call x1, Pallas kernels: 28.6 us -> 28 us  [local(): pl.pallas_call(functools.partial(kernel, n_sh, n_sw, half, hd), out_shape...]
where the time goes in v3:
time: 29.6 us; the launch traced here: 29.5 us
  Pallas kernels  28.8 us (97%)
  between operations  0.64 us (2%)
    pallas_call x1, Pallas kernels, local(): pl.pallas_call(functools.partial(kernel, n_sh, n_sw, half, hd), out_shape...  28 us
    pallas_call x1, Pallas kernels, local(): pl.pallas_call(hand_out, out_shape=[jax.ShapeDtypeStruct((tok, cols), BF)...  0.83 us

profile of v3, /device:TPU:1, one launch (start us, length us, event | category | flops | bytes accessed | tf_op | source)
XLA Modules:
  0.0 29.5 jit_solution(17496682989442901799)
XLA Ops:
  0.6 28.0 %shard_map.94 = (bf16[64,1536]{1,0:T(8,128)(2,1)S(1)}, bf16[64,1536]{1,0:T(8,128)(2,1)S(1)}, bf16[64,1536]{1,0:T(8,128)(2,1)S(1)}) custom-call(bf16[64,1536]{1,0:T(8,128)(2,1)} %bitcast.10, bf16[64,1536]{1,0:T(8,128)(2,1)} %bitcast.11, bf16[64,1536]{1,0:T(8,128)(2,1)} %bitcast.12, bf16[64,1536]{1,0:T(8,128)(2,1)} %bitcast.13, bf16[64,1536]{1,0:T(8,128)(2,1)} %bitcast.14, ...), custom_call_target="tpu_custom_call" | custom-call | tf_op jit(solution)/shard_map/pallas_call | solution.py:417
  28.6 0.8 %shard_map.95 = (bf16[64,1536]{1,0:T(8,128)(2,1)}, bf16[64,1536]{1,0:T(8,128)(2,1)}, bf16[64,1536]{1,0:T(8,128)(2,1)}) custom-call(bf16[64,1536]{1,0:T(8,128)(2,1)S(1)} %get-tuple-element.9.a_in, bf16[64,1536]{1,0:T(8,128)(2,1)S(1)} %get-tuple-element.10.b_in, bf16[64,1536]{1,0:T(8,128)(2,1)S(1)} %get-tuple-element.11.c_in), custom_call_target="tpu_custom_call" | custom-call | tf_op jit(solution)/shard_map/pallas_call | solution.py:427

commit v4 on v3

--- a/solution.py
+++ b/solution.py
@@ -281,13 +281,16 @@
                     if run == 0:
                         drain(stats.at[0:1 + v], wtr.at[c])
 
-    def batch(run, k):
-        for h in range(*spans[k]):
+    def nears(run, *heads):
+        for h in heads:
             near(run, h)
+        for h in heads:
             copy_xback(run, h).start()
+
+    def back(run, k):
         for e in SIDES:
             dqs[run * 9 + e, k] = dqp[src_of[(run * 9 + e) * third + k]]
-
+        for e in SIDES:
             @pl.when(came_from(e))
             def _():
                 copy_back(run, e, k).start()
@@ -318,21 +321,30 @@
 
     loads[2].wait()
     loads[3].wait()
-    for k in range(third):
-        relay(0, k)
+    relay(0, 0)
+    relay(0, 1)
+    relay(0, 2)
     got_x(0)
     own(0)
     relay(1, 0)
     arrived(0)
-    for k in range(third):
-        batch(0, k)
-    for k in range(1, third):
-        relay(1, k)
+    nears(0,0,1)
+    relay(1,1)
+    nears(0,2,3)
+    relay(1,2)
+    nears(0,4,5)
+    back(0, 0)
+    back(0, 1)
+    back(0, 2)
     got_x(1)
     own(1)
     arrived(1)
-    for k in range(third):
-        batch(1, k)
+    nears(1, 0, 1)
+    nears(1, 2, 3)
+    back(1, 0)
+    nears(1, 4, 5)
+    back(1, 1)
+    back(1, 2)
     finish_kv(0)
     finish_q(0)
     finish_kv(1)

time: 29.6 us -> 27.4 us (0.926); the launches traced: 29.5 us -> 27 us
  Pallas kernels: 28.8 us -> 26.3 us
    pallas_call x1, Pallas kernels: 28 us -> 25.5 us  [local(): pl.pallas_call(functools.partial(kernel, n_sh, n_sw, half, hd), out_shape...]
where the time goes in v4:
time: 27.4 us; the launch traced here: 27 us
  Pallas kernels  26.3 us (96%)
  between operations  0.64 us (2%)
    pallas_call x1, Pallas kernels, local(): pl.pallas_call(functools.partial(kernel, n_sh, n_sw, half, hd), out_shape...  25.5 us
    pallas_call x1, Pallas kernels, local(): pl.pallas_call(hand_out, out_shape=[jax.ShapeDtypeStruct((tok, cols), BF)...  0.83 us

profile of v4, /device:TPU:1, one launch (start us, length us, event | category | flops | bytes accessed | tf_op | source)
XLA Modules:
  0.0 27.0 jit_solution(1090279683423097807)
XLA Ops:
  0.6 25.5 %shard_map.94 = (bf16[64,1536]{1,0:T(8,128)(2,1)S(1)}, bf16[64,1536]{1,0:T(8,128)(2,1)S(1)}, bf16[64,1536]{1,0:T(8,128)(2,1)S(1)}) custom-call(bf16[64,1536]{1,0:T(8,128)(2,1)} %bitcast.10, bf16[64,1536]{1,0:T(8,128)(2,1)} %bitcast.11, bf16[64,1536]{1,0:T(8,128)(2,1)} %bitcast.12, bf16[64,1536]{1,0:T(8,128)(2,1)} %bitcast.13, bf16[64,1536]{1,0:T(8,128)(2,1)} %bitcast.14, ...), custom_call_target="tpu_custom_call" | custom-call | tf_op jit(solution)/shard_map/pallas_call | solution.py:429
  26.1 0.8 %shard_map.95 = (bf16[64,1536]{1,0:T(8,128)(2,1)}, bf16[64,1536]{1,0:T(8,128)(2,1)}, bf16[64,1536]{1,0:T(8,128)(2,1)}) custom-call(bf16[64,1536]{1,0:T(8,128)(2,1)S(1)} %get-tuple-element.9.a_in, bf16[64,1536]{1,0:T(8,128)(2,1)S(1)} %get-tuple-element.10.b_in, bf16[64,1536]{1,0:T(8,128)(2,1)S(1)} %get-tuple-element.11.c_in), custom_call_target="tpu_custom_call" | custom-call | tf_op jit(solution)/shard_map/pallas_call | solution.py:439

commit v5 on v4

--- a/solution.py
+++ b/solution.py
@@ -23,18 +23,18 @@
     n_sh, n_sw, half, hd,
     q_in, k_in, v_in, g_in, o_in, lse_in, wd_in,
     dq_out, dk_out, dv_out,
-    kvx, qg, zq, pieces0, pieces1, packed, stats,
+    kvx, qg, zq, packed, stats,
     q_ref, k_ref, v_ref, g_ref, o_ref, lse_ref, wd_ref, in_sem,
     dqp, dqs, dqr0, dqr1, own_kv, own_q, xsend, xback,
-    head_of, src_of, flat_of, e_of,
+    head_of, src_of, flat_of, e_of, rank_of,
     zs, zr, zts, ztr, xs, xr, ws, wr, wts, wtr, bs, br, rxr, *zbs,
 ):
     row = lax.axis_index("sh")
     col = lax.axis_index("sw")
     part = lax.axis_index("tp")
-    pieces = (pieces0, pieces1)
     dqr = (dqr0, dqr1)
     third = half // 2
+    pieces = (zbs[4 * third:5 * third], zbs[5 * third:])
     zb = [[zbs[(run * 2 + i) * third:(run * 2 + i + 1) * third] for i in (0, 1)] for run in (0, 1)]
     tok = q_ref.shape[0]
     arguments = (
@@ -73,10 +73,8 @@
         return remote((k_in, v_in)[a].at[:, cols], kvx.at[a, :, cols], xs.at[0], xr.at[run], {"tp": 1 - part})
 
     def copy_w(run, e, k):
-        span = pl.ds(k, 1) if e % 3 else pl.ds(0, third)
-        at = pl.ds(e * third + k, 1) if e % 3 else pl.ds(e * third, third)
         return remote(
-            packed.at[run, e, span], pieces[run].at[at], ws.at[e // 3], wr.at[run, e // 3], {"sw": col + COL_STEP[e // 3]},
+            packed.at[run, e, k], pieces[run][k].at[e], ws.at[e // 3], wr.at[run, e // 3, k], {"sw": col + COL_STEP[e // 3]},
         )
 
     def copy_wstat(e):
@@ -141,6 +139,7 @@
                 e = jnp.where(over == 1, 6, jnp.where(over == 2, 3, 0)) + jnp.where(up == 1, 0, jnp.where(up == 2, 2, 1))
                 flat_of[(run * half + h) * 4 + j] = e * third + rank
                 e_of[(run * half + h) * 4 + j] = e
+                rank_of[(run * half + h) * 4 + j] = rank
                 for s in range(third):
                     mine = jnp.where(here[s], one[j], 0)
                     if h:
@@ -174,7 +173,7 @@
         h = head_of[(run * 9 + e) * third + s]
         block = zq[run * 2 + i - 1, h] if i else qg[run, h]
         if e // 3 == 2:
-            pieces[run][e * third + s] = block
+            pieces[run][s][e] = block
         else:
             packed[run, e, s] = block
 
@@ -189,7 +188,7 @@
             def _():
                 for s in range(third):
                     pack(run, e, s)
-                copy_w(run, e, 0).start()
+                    copy_w(run, e, s).start()
     for e in (0, 3):
         @pl.when(sent_to(e))
         def _():
@@ -200,7 +199,8 @@
         def _():
             stats[e] = jnp.zeros(stats.shape[1:], F32)
             for run in (0, 1):
-                pieces[run][e * third:(e + 1) * third] = jnp.zeros((third,) + pieces0.shape[1:], BF)
+                for k in range(third):
+                    pieces[run][k][e] = jnp.zeros(packed.shape[3:], BF)
 
         @pl.when(jnp.logical_not(sent_to(e)))
         def _():
@@ -227,70 +227,77 @@
                             copy_wstat(e).start()
                 pack(run, 6 + i, k)
 
-    def products(keys, vals, q, g, lse, delta):
-        scores = lax.dot_general(keys, q, NT, preferred_element_type=F32)
-        prob = jnp.exp(scores * scale - lse)
-        grad_prob = lax.dot_general(vals, g, NT, preferred_element_type=F32)
-        score_bf = (prob * (grad_prob - delta)).astype(BF)
-        dv = jnp.dot(prob.astype(BF), g, preferred_element_type=F32)
-        dk = jnp.dot(score_bf, q, preferred_element_type=F32) * scale
-        dq = lax.dot_general(score_bf, keys, TN, preferred_element_type=F32) * scale
-        return dq, dk, dv
+    def products(sets):
+        scores = [lax.dot_general(keys, q, NT, preferred_element_type=F32) for keys, _, q, _, _, _ in sets]
+        grad_prob = [lax.dot_general(vals, g, NT, preferred_element_type=F32) for _, vals, _, g, _, _ in sets]
+        prob = [jnp.exp(score * scale - part[4]) for score, part in zip(scores, sets)]
+        score_bf = [(p * (grad - part[5])).astype(BF) for p, grad, part in zip(prob, grad_prob, sets)]
+        dv = [jnp.dot(p.astype(BF), part[3], preferred_element_type=F32) for p, part in zip(prob, sets)]
+        dk = [jnp.dot(score, part[2], preferred_element_type=F32) * scale for score, part in zip(score_bf, sets)]
+        dq = [lax.dot_general(score, part[0], TN, preferred_element_type=F32) * scale for score, part in zip(score_bf, sets)]
+        return zip(dq, dk, dv)
 
     def keys_of(at):
         cols = slice(at * hd, (at + 1) * hd)
         return (jnp.concatenate([mine[:, cols], other[:, cols]], axis=0) for mine, other in ((k_ref, kvx.at[0]), (v_ref, kvx.at[1])))
 
     def own(run):
-        for h in range(half):
-            at = run * half + h
-            cols = slice(at * hd, (at + 1) * hd)
-            stat = stats[6, at:at + 1, :]
-            dq, dk, dv = products(
-                *keys_of(at), q_ref[:, cols], g_ref[:, cols], stat[:, :tok], pltpu.roll(stat, tok, 1)[:, :tok],
-            )
-            own_q[at] = dq
-            own_kv[at, 0] = dk
-            own_kv[at, 1] = dv
+        for lo in range(0, half, 3):
+            heads = range(run * half + lo, run * half + min(lo + 3, half))
+            sets = []
+            for at in heads:
+                cols = slice(at * hd, (at + 1) * hd)
+                stat = stats[6, at:at + 1, :]
+                sets.append((*keys_of(at), q_ref[:, cols], g_ref[:, cols], stat[:, :tok], pltpu.roll(stat, tok, 1)[:, :tok]))
+            for at, (dq, dk, dv) in zip(heads, products(sets)):
+                own_q[at] = dq
+                own_kv[at, 0] = dk
+                own_kv[at, 1] = dv
 
     first = lax.broadcasted_iota(jnp.int32, (1, hd), 1) < tok
 
-    def near(run, h):
+    def parts_of(run, h):
         at = run * half + h
-        where = [flat_of[at * 4 + j] for j in range(4)]
-        q = jnp.concatenate([pieces[run][w, 0] for w in where], axis=0)
-        g = jnp.concatenate([pieces[run][w, 1] for w in where], axis=0)
+        blocks = []
+        for j in range(4):
+            e = e_of[at * 4 + j]
+            block = pieces[run][0][e]
+            for k in range(1, min(h, third - 1) + 1):
+                block = jnp.where(rank_of[at * 4 + j] == k, pieces[run][k][e], block)
+            blocks.append(block)
+        q = jnp.concatenate([block[0] for block in blocks], axis=0)
+        g = jnp.concatenate([block[1] for block in blocks], axis=0)
         stat = [stats[e_of[at * 4 + j], at:at + 1, :] for j in range(4)]
         turn = [pltpu.roll(s, tok, 1) for s in stat]
         lse = jnp.concatenate([jnp.where(first, stat[j], turn[j + 1]) for j in (0, 2)], axis=1)
         delta = jnp.concatenate([jnp.where(first, turn[j], stat[j + 1]) for j in (0, 2)], axis=1)
-        dq, dk, dv = products(*keys_of(at), q, g, lse, delta)
-        for j in range(4):
-            dqp[at * 4 + j] = dq[j * tok:(j + 1) * tok].astype(BF)
-        for a, grad in ((0, dk), (1, dv)):
-            total = own_kv[at, a] + grad
-            own_kv[at, a, :tok] = total[:tok]
-            xsend[run, h, a] = total[tok:].astype(BF)
-
-    def arrived(run):
+        return (*keys_of(at), q, g, lse, delta)
+
+    def arrived(run, k):
         for c in (0, 1):
             for v in (0, 1, 2):
                 @pl.when(col_ok(-COL_STEP[c]) & (n_rows == v))
                 def _():
-                    drain(pieces[run].at[0:third * (1 + v)], wr.at[run, c])
-                    if run == 0:
+                    drain(pieces[run][k].at[0:1 + v], wr.at[run, c, k])
+                    if run == 0 and k == 0:
                         drain(stats.at[0:1 + v], wtr.at[c])
 
     def nears(run, *heads):
-        for h in heads:
-            near(run, h)
+        for h, (dq, dk, dv) in zip(heads, products([parts_of(run, h) for h in heads])):
+            at = run * half + h
+            for a, grad in ((0, dk), (1, dv)):
+                total = own_kv[at, a] + grad
+                own_kv[at, a, :tok] = total[:tok]
+                xsend[run, h, a] = total[tok:].astype(BF)
+            for j in range(4):
+                dqp[at * 4 + j] = dq[j * tok:(j + 1) * tok].astype(BF)
         for h in heads:
             copy_xback(run, h).start()
 
-    def back(run, k):
-        for e in SIDES:
+    def back(run, k, some=SIDES):
+        for e in some:
             dqs[run * 9 + e, k] = dqp[src_of[(run * 9 + e) * third + k]]
-        for e in SIDES:
+        for e in some:
             @pl.when(came_from(e))
             def _():
                 copy_back(run, e, k).start()
@@ -326,25 +333,36 @@
     relay(0, 2)
     got_x(0)
     own(0)
-    relay(1, 0)
-    arrived(0)
-    nears(0,0,1)
+    arrived(0,0)
+    nears(0,0)
+    arrived(0,1)
+    nears(0,1)
+    relay(1,0)
+    arrived(0,2)
+    nears(0,2,3)
     relay(1,1)
-    nears(0,2,3)
     relay(1,2)
     nears(0,4,5)
-    back(0, 0)
-    back(0, 1)
-    back(0, 2)
     got_x(1)
     own(1)
-    arrived(1)
-    nears(1, 0, 1)
-    nears(1, 2, 3)
-    back(1, 0)
-    nears(1, 4, 5)
-    back(1, 1)
-    back(1, 2)
+    back(0,0,(7,8,1,2,4,5,0,3))
+    back(0,1,(7,8,1,2,4,5,0,3))
+    back(0,2,(7,8,1,2,4,5,0,3))
+    arrived(1,0)
+    nears(1,0)
+    arrived(1,1)
+    nears(1,1)
+    arrived(1,2)
+    nears(1,2,3,4,5)
+    back(1,0,(1,2,4,5))
+    back(1,1,(1,2,4,5))
+    back(1,2,(1,2,4,5))
+    back(1,0,(7,8))
+    back(1,1,(7,8))
+    back(1,2,(7,8))
+    back(1,0,(0,3))
+    back(1,1,(0,3))
+    back(1,2,(0,3))
     finish_kv(0)
     finish_q(0)
     finish_kv(1)
@@ -400,8 +418,6 @@
             pltpu.VMEM((4, half, 2, tok, hd), BF),
         ]
         + [
-            pltpu.VMEM((9 * third, 2, tok, hd), BF),
-            pltpu.VMEM((9 * third, 2, tok, hd), BF),
             pltpu.VMEM((2, 6, third, 2, tok, hd), BF),
             pltpu.VMEM((9, 16, hd), F32),
         ]
@@ -420,12 +436,14 @@
             pltpu.SMEM((18 * third,), jnp.int32),
             pltpu.SMEM((heads * 4,), jnp.int32),
             pltpu.SMEM((heads * 4,), jnp.int32),
+            pltpu.SMEM((heads * 4,), jnp.int32),
         ]
     )
-    sems = ((2,), (2, 2, third), (2,), (2,), (1,), (2,), (2,), (2, 2), (2,), (2,), (3,), (2, 3), (2,))
+    sems = ((2,), (2, 2, third), (2,), (2,), (1,), (2,), (2,), (2, 2, third), (2,), (2,), (3,), (2, 3), (2,))
     scratch += [dma(sem) for sem in sems]
     for _ in range(4):
         scratch += [pltpu.VMEM((2, tok, (half - third + 1 if k == 0 else 1) * hd), BF) for k in range(third)]
+    scratch += [pltpu.VMEM((9, 2, tok, hd), BF) for _ in range(2 * third)]
     dq, dk, dv = pl.pallas_call(
         functools.partial(kernel, n_sh, n_sw, half, hd),
         out_shape=[pltpu.VMEM((tok, cols), BF)] * 3,

time: 27.4 us -> 26.7 us (0.974); the launches traced: 27 us -> 26.6 us
  Pallas kernels: 26.3 us -> 25.9 us
    pallas_call x1, Pallas kernels: 25.5 us -> 25.1 us  [local(): pl.pallas_call(functools.partial(kernel, n_sh, n_sw, half, hd), out_shape...]
where the time goes in v5:
time: 26.7 us; the launch traced here: 26.6 us
  Pallas kernels  25.9 us (97%)
  between operations  0.64 us (2%)
    pallas_call x1, Pallas kernels, local(): pl.pallas_call(functools.partial(kernel, n_sh, n_sw, half, hd), out_shape...  25.1 us
    pallas_call x1, Pallas kernels, local(): pl.pallas_call(hand_out, out_shape=[jax.ShapeDtypeStruct((tok, cols), BF)...  0.83 us

profile of v5, /device:TPU:1, one launch (start us, length us, event | category | flops | bytes accessed | tf_op | source)
XLA Modules:
  0.0 26.6 jit_solution(7554414004073322803)
XLA Ops:
  0.6 25.1 %shard_map.94 = (bf16[64,1536]{1,0:T(8,128)(2,1)S(1)}, bf16[64,1536]{1,0:T(8,128)(2,1)S(1)}, bf16[64,1536]{1,0:T(8,128)(2,1)S(1)}) custom-call(bf16[64,1536]{1,0:T(8,128)(2,1)} %bitcast.10, bf16[64,1536]{1,0:T(8,128)(2,1)} %bitcast.11, bf16[64,1536]{1,0:T(8,128)(2,1)} %bitcast.12, bf16[64,1536]{1,0:T(8,128)(2,1)} %bitcast.13, bf16[64,1536]{1,0:T(8,128)(2,1)} %bitcast.14, ...), custom_call_target="tpu_custom_call" | custom-call | tf_op jit(solution)/shard_map/pallas_call | solution.py:447
  25.7 0.8 %shard_map.95 = (bf16[64,1536]{1,0:T(8,128)(2,1)}, bf16[64,1536]{1,0:T(8,128)(2,1)}, bf16[64,1536]{1,0:T(8,128)(2,1)}) custom-call(bf16[64,1536]{1,0:T(8,128)(2,1)S(1)} %get-tuple-element.9.a_in, bf16[64,1536]{1,0:T(8,128)(2,1)S(1)} %get-tuple-element.10.b_in, bf16[64,1536]{1,0:T(8,128)(2,1)S(1)} %get-tuple-element.11.c_in), custom_call_target="tpu_custom_call" | custom-call | tf_op jit(solution)/shard_map/pallas_call | solution.py:457

commit v6 on v5

--- a/solution.py
+++ b/solution.py
@@ -41,8 +41,6 @@
         (q_in, q_ref), (g_in, g_ref), (k_in, k_ref), (v_in, v_ref), (wd_in, wd_ref), (o_in, o_ref), (lse_in, lse_ref),
     )
     loads = [pltpu.make_async_copy(src, dst, in_sem.at[i]) for i, (src, dst) in enumerate(arguments)]
-    for load in loads:
-        load.start()
     scale = hd ** -0.5
     row_ok = lambda step: (row + step >= 0) & (row + step < n_sh)
     col_ok = lambda step: (col + step >= 0) & (col + step < n_sw)
@@ -104,17 +102,19 @@
             pl.semaphore_signal(barrier, inc=1, device_id=near, device_id_type=MESH)
         count = count + sent_to(e).astype(jnp.int32)
 
+    for load in loads:
+        load.start()
     pl.semaphore_wait(barrier, count)
 
-    def send_z(run):
-        for k in range(third):
+    def send_z(run, *chunks):
+        for k in chunks:
             for i in (0, 1):
                 @pl.when(row_ok(2 * i - 1))
                 def _():
                     copy_z(run, i, k, 0).start()
                     copy_z(run, i, k, 1).start()
 
-    send_z(0)
+    send_z(0, *range(third - 1))
     for run in (0, 1):
         for a in (0, 1):
             copy_x(run, a).start()
@@ -166,7 +166,8 @@
         @pl.when(row_ok(2 * i - 1))
         def _():
             copy_zstat(i).start()
-    send_z(1)
+    send_z(0, third - 1)
+    send_z(1, *range(third))
 
     def pack(run, e, s):
         i = e % 3
@@ -216,14 +217,14 @@
                 for n, h in enumerate(range(*spans[k])):
                     for a in (0, 1):
                         zq[run * 2 + i - 1, h, a] = held[a, :, n * hd:(n + 1) * hd]
-                if run == 0 and k == third - 1:
+                if run == 0 and k == third - 2:
                     copy_zstat(i - 1).wait_recv()
                 for e in (i, 3 + i):
                     @pl.when(col_ok(COL_STEP[e // 3]))
                     def _():
                         pack(run, e, k)
                         copy_w(run, e, k).start()
-                        if run == 0 and k == third - 1:
+                        if run == 0 and k == third - 2:
                             copy_wstat(e).start()
                 pack(run, 6 + i, k)
 

time: 26.7 us -> 26.2 us (0.981)
  Pallas kernels: 25.9 us -> 25.2 us
    pallas_call x1, Pallas kernels: 25.1 us -> 24.4 us  [local(): pl.pallas_call(functools.partial(kernel, n_sh, n_sw, half, hd), out_shape...]
where the time goes in v6:
time: 26.2 us; the launch traced here: 25.9 us
  Pallas kernels  25.2 us (96%)
  between operations  0.64 us (2%)
    pallas_call x1, Pallas kernels, local(): pl.pallas_call(functools.partial(kernel, n_sh, n_sw, half, hd), out_shape...  24.4 us
    pallas_call x1, Pallas kernels, local(): pl.pallas_call(hand_out, out_shape=[jax.ShapeDtypeStruct((tok, cols), BF)...  0.83 us

profile of v6, /device:TPU:1, one launch (start us, length us, event | category | flops | bytes accessed | tf_op | source)
XLA Modules:
  0.0 25.9 jit_solution(14505867542155758199)
XLA Ops:
  0.6 24.4 %shard_map.94 = (bf16[64,1536]{1,0:T(8,128)(2,1)S(1)}, bf16[64,1536]{1,0:T(8,128)(2,1)S(1)}, bf16[64,1536]{1,0:T(8,128)(2,1)S(1)}) custom-call(bf16[64,1536]{1,0:T(8,128)(2,1)} %bitcast.10, bf16[64,1536]{1,0:T(8,128)(2,1)} %bitcast.11, bf16[64,1536]{1,0:T(8,128)(2,1)} %bitcast.12, bf16[64,1536]{1,0:T(8,128)(2,1)} %bitcast.13, bf16[64,1536]{1,0:T(8,128)(2,1)} %bitcast.14, ...), custom_call_target="tpu_custom_call" | custom-call | tf_op jit(solution)/shard_map/pallas_call | solution.py:448
  25.0 0.8 %shard_map.95 = (bf16[64,1536]{1,0:T(8,128)(2,1)}, bf16[64,1536]{1,0:T(8,128)(2,1)}, bf16[64,1536]{1,0:T(8,128)(2,1)}) custom-call(bf16[64,1536]{1,0:T(8,128)(2,1)S(1)} %get-tuple-element.9.a_in, bf16[64,1536]{1,0:T(8,128)(2,1)S(1)} %get-tuple-element.10.b_in, bf16[64,1536]{1,0:T(8,128)(2,1)S(1)} %get-tuple-element.11.c_in), custom_call_target="tpu_custom_call" | custom-call | tf_op jit(solution)/shard_map/pallas_call | solution.py:458

commit v7 on v6

--- a/solution.py
+++ b/solution.py
@@ -84,7 +84,7 @@
         return remote(dqs.at[at, k], dqr[run].at[e * third + k], bs.at[e % 3], br.at[run, e % 3], home)
 
     def copy_xback(run, h):
-        return remote(xsend.at[run, h], xback.at[run, h], xs.at[0], rxr.at[run], {"tp": 1 - part})
+        return remote(xsend.at[run, h], xback.at[run, h], xs.at[0], rxr.at[run, int(h >= half - 1)], {"tp": 1 - part})
 
     n_rows = row_ok(-1).astype(jnp.int32) + row_ok(1).astype(jnp.int32)
     n_cols = col_ok(-1).astype(jnp.int32) + col_ok(1).astype(jnp.int32)
@@ -226,6 +226,9 @@
                         copy_w(run, e, k).start()
                         if run == 0 and k == third - 2:
                             copy_wstat(e).start()
+        for i in (1, 2):
+            @pl.when(row_ok(-ROW_STEP[i]))
+            def _():
                 pack(run, 6 + i, k)
 
     def products(sets):
@@ -304,8 +307,10 @@
                 copy_back(run, e, k).start()
 
     def finish_kv(run):
-        drain(xback.at[run], rxr.at[run])
+        drain(xback.at[run, 0:half - 1], rxr.at[run, 0])
         for h in range(half):
+            if h == half - 1:
+                drain(xback.at[run, h], rxr.at[run, 1])
             cols = slice((run * half + h) * hd, (run * half + h + 1) * hd)
             for a, out in ((0, dk_out), (1, dv_out)):
                 out[:, cols] = (own_kv[run * half + h, a, :tok] + xback[run, h, a].astype(F32)).astype(BF)
@@ -366,8 +371,8 @@
     back(1,2,(0,3))
     finish_kv(0)
     finish_q(0)
+    finish_q(1)
     finish_kv(1)
-    finish_q(1)
 
     drain(dqp, xs.at[0])
     for i in (0, 1):
@@ -440,7 +445,7 @@
             pltpu.SMEM((heads * 4,), jnp.int32),
         ]
     )
-    sems = ((2,), (2, 2, third), (2,), (2,), (1,), (2,), (2,), (2, 2, third), (2,), (2,), (3,), (2, 3), (2,))
+    sems = ((2,), (2, 2, third), (2,), (2,), (1,), (2,), (2,), (2, 2, third), (2,), (2,), (3,), (2, 3), (2, 2))
     scratch += [dma(sem) for sem in sems]
     for _ in range(4):
         scratch += [pltpu.VMEM((2, tok, (half - third + 1 if k == 0 else 1) * hd), BF) for k in range(third)]

time: 26.2 us -> 26.1 us (level)
  no operation moved by 1% of the time
where the time goes in v7:
time: 26.1 us; the launch traced here: 25.9 us
  Pallas kernels  25.3 us (97%)
  between operations  0.64 us (2%)
    pallas_call x1, Pallas kernels, local(): pl.pallas_call(functools.partial(kernel, n_sh, n_sw, half, hd), out_shape...  24.5 us
    pallas_call x1, Pallas kernels, local(): pl.pallas_call(hand_out, out_shape=[jax.ShapeDtypeStruct((tok, cols), BF)...  0.83 us

profile of v7, /device:TPU:1, one launch (start us, length us, event | category | flops | bytes accessed | tf_op | source)
XLA Modules:
  0.0 25.9 jit_solution(336633829835320472)
XLA Ops:
  0.6 24.5 %shard_map.94 = (bf16[64,1536]{1,0:T(8,128)(2,1)S(1)}, bf16[64,1536]{1,0:T(8,128)(2,1)S(1)}, bf16[64,1536]{1,0:T(8,128)(2,1)S(1)}) custom-call(bf16[64,1536]{1,0:T(8,128)(2,1)} %bitcast.10, bf16[64,1536]{1,0:T(8,128)(2,1)} %bitcast.11, bf16[64,1536]{1,0:T(8,128)(2,1)} %bitcast.12, bf16[64,1536]{1,0:T(8,128)(2,1)} %bitcast.13, bf16[64,1536]{1,0:T(8,128)(2,1)} %bitcast.14, ...), custom_call_target="tpu_custom_call" | custom-call | tf_op jit(solution)/shard_map/pallas_call | solution.py:453
  25.1 0.8 %shard_map.95 = (bf16[64,1536]{1,0:T(8,128)(2,1)}, bf16[64,1536]{1,0:T(8,128)(2,1)}, bf16[64,1536]{1,0:T(8,128)(2,1)}) custom-call(bf16[64,1536]{1,0:T(8,128)(2,1)S(1)} %get-tuple-element.9.a_in, bf16[64,1536]{1,0:T(8,128)(2,1)S(1)} %get-tuple-element.10.b_in, bf16[64,1536]{1,0:T(8,128)(2,1)S(1)} %get-tuple-element.11.c_in), custom_call_target="tpu_custom_call" | custom-call | tf_op jit(solution)/shard_map/pallas_call | solution.py:463
